TPU v7x, 32 devices: a whole 2x2x4 slice. The times are simulated.
32 devices in a mesh: parts: 2 (over x), src: 8 (over z, y), tile: 2 (over core).
Axes of the slice: x: 2, y: 2, z: 4, core: 2. Of those that a mesh axis runs over, the one named last changes fastest.
Arguments:
- mask_values: bfloat16 [2048, 512], P(('parts', 'tile')), parts along dimension 0, may hold values from -1 to 1
- target_image: float32 [2048, 512], P(('parts', 'tile')), parts along dimension 0, may hold values from 0 to 1.5
- jones_pupil: float32 [2, 3, 2, 128, 128], replicated, may hold values from -1.7 to 1.7
- polar_states: float32 [4, 2, 2], replicated, may hold values from -3 to 3
- source_weights: float32 [64], P(('parts', 'src')), parts along dimension 0, may hold values from 0.25 to 4
- pupil_offsets: int32 [64, 2], P(('parts', 'src')), parts along dimension 0, may hold values from 0 to 64
- polar_ids: int32 [64], P(('parts', 'src')), parts along dimension 0, may hold values from 0 to 3
Outputs:
- intensity: float32 [4, 512, 512], P(('parts', 'tile'), 'src'), parts along dimension 0
- mask_grad: float32 [4, 512, 512], P(('parts', 'tile'), 'src'), parts along dimension 0
- source_grad: float32 [64], P(('parts', 'src')), parts along dimension 0
There are 2 independent parts, one for each index of `parts`. A program takes and returns all parts, laid end to end along the dimension named above; an argument that names none is the same for every part. Nothing has to cross between parts.
All inputs are finite; a program needn't handle non-finite values.
Results may differ from a plain program's by a relative error of at most 0.018.
Values may be sent and summed in bfloat16 or wider, within the bound.
A program may use at most 64 MiB of HBM per device.

v0:
```python
import math

import jax
import jax.numpy as jnp
from jax import lax
from jax.sharding import PartitionSpec as P

TH = 512
TW = 512
AMB = 64
K = 64
NPOL = 4


TWO_PI = 2.0 * math.pi
GRAD_SCALE = 32.0


def with_halo(cells, sides, width):
    for axis, dim in sides:
        count = lax.axis_size(axis)
        ends = count - 1
        head = lax.slice_in_dim(cells, 0, width, axis=dim)
        tail = lax.slice_in_dim(cells, cells.shape[dim] - width, cells.shape[dim], axis=dim)
        cells = jnp.concatenate(
            [
                lax.ppermute(tail, axis, [(i, (i + 1) % count) for i in range(ends)]),
                cells,
                lax.ppermute(head, axis, [((i + 1) % count, i) for i in range(ends)]),
            ],
            axis=dim,
        )
    return cells


def partner(value, axis, apart):
    mask = 2**apart
    pairs = [(source, source ^ mask) for source in range(lax.axis_size(axis))]
    return lax.ppermute(value, axis, pairs)


def tables():
    window = TH + 2 * AMB
    orders = jnp.arange(K, dtype=jnp.int32) - K // 2
    columns = jnp.arange(TW, dtype=jnp.int32)
    win_rows = jnp.arange(window, dtype=jnp.int32)
    core_rows = jnp.arange(TH, dtype=jnp.int32) + AMB
    col_angle = TWO_PI * jnp.mod(columns[:, None] * orders[None, :], TW).astype(jnp.float32) / TW
    row_angle = (
        TWO_PI * jnp.mod(orders[:, None] * win_rows[None, :], window).astype(jnp.float32) / window
    )
    core_angle = (
        TWO_PI * jnp.mod(core_rows[:, None] * orders[None, :], window).astype(jnp.float32) / window
    )
    col_fwd = jnp.concatenate([jnp.cos(col_angle), -jnp.sin(col_angle)], 1).astype(jnp.bfloat16)
    row_fwd = jnp.concatenate([jnp.cos(row_angle), jnp.sin(row_angle)], 0).astype(jnp.bfloat16)
    upper_rows = jnp.concatenate([jnp.cos(core_angle), -jnp.sin(core_angle)], 1)
    lower_rows = jnp.concatenate([jnp.sin(core_angle), jnp.cos(core_angle)], 1)
    row_inv = jnp.concatenate([upper_rows, lower_rows], 0).astype(jnp.bfloat16)
    cos_cols = jnp.cos(col_angle).T
    sin_cols = jnp.sin(col_angle).T
    col_inv = jnp.concatenate(
        [jnp.concatenate([cos_cols, sin_cols], 1), jnp.concatenate([-sin_cols, cos_cols], 1)], 0
    ).astype(jnp.bfloat16)
    return (col_fwd, row_fwd, row_inv, col_inv)


def spectrum(extended, col_fwd, row_fwd):
    partial_dft = jnp.dot(extended, col_fwd, preferred_element_type=jnp.float32).astype(
        jnp.bfloat16
    )
    product = jnp.dot(row_fwd, partial_dft, preferred_element_type=jnp.float32)
    norm_scale = 1.0 / math.sqrt((TH + 2 * AMB) * TW)
    spectrum_re = norm_scale * (product[:K, :K] + product[K:, K:])
    spectrum_im = norm_scale * (product[:K, K:] - product[K:, :K])
    return (spectrum_re, spectrum_im)


def pupil_of(jones_pupil, polar_states, offset, state_id):
    one_hot = (jnp.arange(NPOL, dtype=jnp.int32) == state_id).astype(jnp.float32)
    jones_vec = jnp.sum(one_hot[:, None, None] * polar_states, 0)
    zero_index = jnp.zeros((), jnp.int32)
    window = lax.dynamic_slice(
        jones_pupil, (zero_index, zero_index, zero_index, offset[0], offset[1]), (2, 3, 2, K, K)
    )
    vec_re = jones_vec[0][None, :, None, None]
    vec_im = jones_vec[1][None, :, None, None]
    pupil_re = jnp.sum(window[0] * vec_re - window[1] * vec_im, 1)
    pupil_im = jnp.sum(window[0] * vec_im + window[1] * vec_re, 1)
    return (pupil_re, pupil_im)


def masked_stack(pupil_re, pupil_im, spectrum_re, spectrum_im):
    masked_re = pupil_re * spectrum_re - pupil_im * spectrum_im
    masked_im = pupil_re * spectrum_im + pupil_im * spectrum_re
    return jnp.concatenate([masked_re, masked_im], 1).astype(jnp.bfloat16)


def row_field_of(stacked, row_inv):
    half_rows = row_inv.shape[0] // 2
    rows_out = jnp.einsum("ak,ckl->cal", row_inv, stacked, preferred_element_type=jnp.float32)
    return jnp.concatenate([rows_out[:, :half_rows], rows_out[:, half_rows:]], 2).astype(
        jnp.bfloat16
    )


def field_of(row_field, col_inv):
    return jnp.einsum("cpk,kq->cpq", row_field, col_inv, preferred_element_type=jnp.float32) / K


def intensity_of(field):
    return jnp.sum(field[..., :TW] * field[..., :TW] + field[..., TW:] * field[..., TW:], 0)


def adjoint_terms(field, residual, weight, pupil_re, pupil_im, row_inv, col_inv, source_total):
    coefficient = 2.0 * weight / (source_total * K)
    doubled = jnp.concatenate([residual, residual], 1)
    field_grad = (coefficient * doubled[None] * field).astype(jnp.bfloat16)
    row_grad = jnp.einsum(
        "cpq,kq->cpk", field_grad, col_inv, preferred_element_type=jnp.float32
    ).astype(jnp.bfloat16)
    stacked = jnp.concatenate([row_grad[..., :K], row_grad[..., K:]], 1)
    masked_grad = jnp.einsum("ak,cal->ckl", row_inv, stacked, preferred_element_type=jnp.float32)
    grad_re = masked_grad[:, :K]
    grad_im = masked_grad[:, K:]
    spec_re = jnp.sum(pupil_re * grad_re + pupil_im * grad_im, 0)
    spec_im = jnp.sum(pupil_re * grad_im - pupil_im * grad_re, 0)
    return (spec_re, spec_im)


def window_grad(grad_re, grad_im, row_fwd, col_fwd):
    norm_scale = 1.0 / math.sqrt((TH + 2 * AMB) * TW)
    top_rows = jnp.concatenate([grad_re, grad_im], 1)
    bottom_rows = jnp.concatenate([-grad_im, grad_re], 1)
    grad_prod = norm_scale * jnp.concatenate([top_rows, bottom_rows], 0)
    grad_partial = jnp.dot(
        row_fwd.astype(jnp.float32).T, grad_prod, precision=lax.Precision.HIGHEST
    )
    return jnp.dot(grad_partial, col_fwd.astype(jnp.float32).T, precision=lax.Precision.HIGHEST)


def body(
    mask_values, target_image, jones_pupil, polar_states, source_weights, pupil_offsets, polar_ids
):
    col_fwd, row_fwd, row_inv, col_inv = tables()
    extended = with_halo(mask_values, (("tile", 0),), AMB)
    spectrum_re, spectrum_im = spectrum(extended, col_fwd, row_fwd)
    src_count = lax.axis_size("src")
    tile_count = lax.axis_size("tile")
    local_count = source_weights.shape[0]
    source_total = local_count * src_count
    row_share = TH // src_count
    row_start = lax.axis_index("src") * row_share
    empty = jnp.zeros((K, K), jnp.float32)

    def forward(running, item):
        weight, offset, state_id = item
        pupil_re, pupil_im = pupil_of(jones_pupil, polar_states, offset, state_id)
        stacked = masked_stack(pupil_re, pupil_im, spectrum_re, spectrum_im)
        row_field = row_field_of(stacked, row_inv)
        field = field_of(row_field, col_inv)
        return (running + weight / source_total * intensity_of(field), row_field)

    partial_image, row_fields = lax.scan(
        forward, jnp.zeros((TH, TW), jnp.float32), (source_weights, pupil_offsets, polar_ids)
    )
    full_image = lax.psum(partial_image.astype(jnp.bfloat16), "src").astype(jnp.float32)
    residual = full_image - target_image
    own_image = lax.dynamic_slice_in_dim(full_image, row_start, row_share, 0)

    def backward(running, item):
        weight, offset, state_id, row_field = item
        pupil_re, pupil_im = pupil_of(jones_pupil, polar_states, offset, state_id)
        field = field_of(row_field, col_inv)
        spec_re, spec_im = adjoint_terms(
            field, residual, weight, pupil_re, pupil_im, row_inv, col_inv, source_total
        )
        return (
            (running[0] + spec_re, running[1] + spec_im),
            jnp.sum(residual * intensity_of(field)),
        )

    (grad_re, grad_im), weight_terms = lax.scan(
        backward, (empty, empty), (source_weights, pupil_offsets, polar_ids, row_fields)
    )
    source_grad = lax.psum(weight_terms, "tile") / (tile_count * TH * TW)
    total_re, total_im = lax.psum((grad_re, grad_im), "src")
    grad_window = window_grad(total_re, total_im, row_fwd, col_fwd)
    is_first = lax.axis_index("tile") == 0
    outgoing = jnp.where(is_first, grad_window[TH + AMB :], grad_window[:AMB])
    incoming = partner(outgoing, "tile", 0)
    zero_rims = jnp.zeros_like(incoming)
    middle_rows = jnp.zeros((TH - 2 * AMB, TW), jnp.float32)
    added_rows = jnp.concatenate(
        [
            jnp.where(is_first, zero_rims, incoming),
            middle_rows,
            jnp.where(is_first, incoming, zero_rims),
        ],
        0,
    )
    core_grad = grad_window[AMB : AMB + TH] + added_rows
    own_grad = GRAD_SCALE * lax.dynamic_slice_in_dim(core_grad, row_start, row_share, 0)
    return (own_image.reshape(1, row_share, TW), own_grad.reshape(1, row_share, TW), source_grad)


def solution(mesh):
    placed = (
        P(("parts", "tile"), None),
        P(("parts", "tile"), None),
        P(),
        P(),
        P(("parts", "src")),
        P(("parts", "src"), None),
        P(("parts", "src")),
    )
    return jax.shard_map(
        body,
        mesh=mesh,
        in_specs=placed,
        out_specs=(
            P(("parts", "tile"), "src", None),
            P(("parts", "tile"), "src", None),
            P(("parts", "src")),
        ),
        check_vma=False,
    )
```

profile of v0, /device:TPU:1, one launch (start us, length us, event | category | flops | bytes accessed | tf_op | source)
XLA Modules:
  0.0 297.8 jit_solution(17822191851575432790)
XLA Ops:
  7.2 0.9 fusion.91
  8.2 2.0 collective-permute-start.1
  10.1 1.3 collective-permute-start
  12.9 1.3 negate_convert_fusion.1
  15.3 47.6 %while.30 = (s32[]{:T(128)}, f32[512,512]{1,0:T(8,128)S(1)}, bf16[4,3,512,128]{2,3,1,0:T(8,128)(2,1)}, f32[4]{0:T(128)S(1)}, s32[4,2]{0,1:T(2,128)S(1)}, /*index...) while((s32[]{:T(128)}, f32[512,512]{1,0:T(8,128)S(1)}, ...), condition=%wide.region_5.6_spmd.clone, body=%wide.region_0.5_spmd.clone.sunk | while | flops 460169248 | bytes 20382208 | solution.py:164
  21.1 1.2 subtract_reduce_fusion.6
  23.0 1.0 broadcast_multiply_fusion.5
  24.0 0.8 fusion.113
  26.4 0.8 maximum_dynamic-update-slice_fusion.2
  33.0 1.2 subtract_reduce_fusion.6
  34.9 1.0 broadcast_multiply_fusion.5
  35.9 0.8 fusion.113
  38.3 0.8 maximum_dynamic-update-slice_fusion.2
  44.9 1.2 subtract_reduce_fusion.6
  46.8 1.0 broadcast_multiply_fusion.5
  47.8 0.8 fusion.113
  50.2 0.8 maximum_dynamic-update-slice_fusion.2
  56.8 1.2 subtract_reduce_fusion.6
  58.7 1.0 broadcast_multiply_fusion.5
  59.7 0.8 fusion.113
  62.1 0.8 maximum_dynamic-update-slice_fusion.2
  62.9 0.9 convert_element_type.87
  63.9 73.8 %all-reduce.3.cloned.1.call-done = bf16[512,512]{1,0:T(8,128)(2,1)} async-done(((bf16[512,512]{1,0:T(8,128)(2,1)}), bf16[512,512]{1,0:T(8,128)(2,1)}) %all-reduce.3.cloned.1.call-update) | async-done | bytes 524304 | tf_op jit(solution)/shard_map/psum | solution.py:167
  137.7 1.2 convert_subtract_fusion
  139.2 104.9 %while.31 = (s32[]{:T(128)}, f32[64,64]{0,1:T(8,128)}, f32[64,64]{0,1:T(8,128)}, f32[4]{0:T(128)}, s32[4,2]{0,1:T(2,128)S(1)}, /*index=5*/f32[2,3,2,128,128]{4,3...) while((s32[]{:T(128)}, f32[64,64]{0,1:T(8,128)}, ...), condition=%wide.region_15.16_spmd.clone, body=%wide.region_7.15_spmd.clone.sunk | while | flops 866074624 | bytes 39519172 | solution.py:183
  145.0 1.9 subtract_reduce_fusion.7
  146.9 1.0 copy.48
  147.9 1.6 copy.49
  149.6 4.7 %broadcast_multiply_fusion.6 = (f32[3,512,1024]{2,1,0:T(8,128)}, f32[3,512,1024]{2,1,0:T(8,128)S(1)}) fusion(bf16[128,1024]{1,0:T(8,128)(2,1)S(1)} %get-tuple-element.800, bf16[4,3,512,128]{2,3,1,0:T(8,128)(2,1)} %get-tuple-element.799, s32[]{:T(128)S(6)} %copy.66), kind=kOutput, calls=%fused_computation.37.clone.1 | convolution fusion | flops 404226048 | bytes 13238276 | tf_op jit(solution)/shard_map/while/body/eval_jaxpr/cpk,kq->cpq/dot_general | solution.py:108
  155.7 1.2 fusion.118
  157.9 1.4 select_add_fusion.6
  159.3 3.8 %fusion.120 = f32[512,512]{1,0:T(8,128)S(1)} fusion(f32[3,512,1024]{2,1,0:T(8,128)} %get-tuple-element.701), kind=kLoop, calls=%fused_computation.35.clone.1 | loop fusion | flops 2883584 | bytes 7340032 | tf_op jit(solution)/shard_map/while/body/eval_jaxpr/reduce_sum | solution.py:112
  163.1 0.9 multiply_reduce_fusion.8
  164.1 0.8 dynamic_update_slice.17
  171.2 1.9 subtract_reduce_fusion.7
  173.1 1.0 copy.48
  174.1 1.6 copy.49
  175.8 4.7 %broadcast_multiply_fusion.6 = (f32[3,512,1024]{2,1,0:T(8,128)}, f32[3,512,1024]{2,1,0:T(8,128)S(1)}) fusion(bf16[128,1024]{1,0:T(8,128)(2,1)S(1)} %get-tuple-element.800, bf16[4,3,512,128]{2,3,1,0:T(8,128)(2,1)} %get-tuple-element.799, s32[]{:T(128)S(6)} %copy.66), kind=kOutput, calls=%fused_computation.37.clone.1 | convolution fusion | flops 404226048 | bytes 13238276 | tf_op jit(solution)/shard_map/while/body/eval_jaxpr/cpk,kq->cpq/dot_general | solution.py:108
  181.9 1.2 fusion.118
  184.1 1.4 select_add_fusion.6
  185.6 3.8 %fusion.120 = f32[512,512]{1,0:T(8,128)S(1)} fusion(f32[3,512,1024]{2,1,0:T(8,128)} %get-tuple-element.701), kind=kLoop, calls=%fused_computation.35.clone.1 | loop fusion | flops 2883584 | bytes 7340032 | tf_op jit(solution)/shard_map/while/body/eval_jaxpr/reduce_sum | solution.py:112
  189.4 0.9 multiply_reduce_fusion.8
  190.3 0.8 dynamic_update_slice.17
  197.5 1.9 subtract_reduce_fusion.7
  199.4 1.0 copy.48
  200.4 1.6 copy.49
  202.0 4.7 %broadcast_multiply_fusion.6 = (f32[3,512,1024]{2,1,0:T(8,128)}, f32[3,512,1024]{2,1,0:T(8,128)S(1)}) fusion(bf16[128,1024]{1,0:T(8,128)(2,1)S(1)} %get-tuple-element.800, bf16[4,3,512,128]{2,3,1,0:T(8,128)(2,1)} %get-tuple-element.799, s32[]{:T(128)S(6)} %copy.66), kind=kOutput, calls=%fused_computation.37.clone.1 | convolution fusion | flops 404226048 | bytes 13238276 | tf_op jit(solution)/shard_map/while/body/eval_jaxpr/cpk,kq->cpq/dot_general | solution.py:108
  208.1 1.2 fusion.118
  210.4 1.4 select_add_fusion.6
  211.8 3.8 %fusion.120 = f32[512,512]{1,0:T(8,128)S(1)} fusion(f32[3,512,1024]{2,1,0:T(8,128)} %get-tuple-element.701), kind=kLoop, calls=%fused_computation.35.clone.1 | loop fusion | flops 2883584 | bytes 7340032 | tf_op jit(solution)/shard_map/while/body/eval_jaxpr/reduce_sum | solution.py:112
  215.6 0.9 multiply_reduce_fusion.8
  223.7 1.9 subtract_reduce_fusion.7
  225.6 1.0 copy.48
  226.6 1.6 copy.49
  228.2 4.7 %broadcast_multiply_fusion.6 = (f32[3,512,1024]{2,1,0:T(8,128)}, f32[3,512,1024]{2,1,0:T(8,128)S(1)}) fusion(bf16[128,1024]{1,0:T(8,128)(2,1)S(1)} %get-tuple-element.800, bf16[4,3,512,128]{2,3,1,0:T(8,128)(2,1)} %get-tuple-element.799, s32[]{:T(128)S(6)} %copy.66), kind=kOutput, calls=%fused_computation.37.clone.1 | convolution fusion | flops 404226048 | bytes 13238276 | tf_op jit(solution)/shard_map/while/body/eval_jaxpr/cpk,kq->cpq/dot_general | solution.py:108
  234.4 1.2 fusion.118
  236.6 1.4 select_add_fusion.6
  238.1 3.8 %fusion.120 = f32[512,512]{1,0:T(8,128)S(1)} fusion(f32[3,512,1024]{2,1,0:T(8,128)} %get-tuple-element.701), kind=kLoop, calls=%fused_computation.35.clone.1 | loop fusion | flops 2883584 | bytes 7340032 | tf_op jit(solution)/shard_map/while/body/eval_jaxpr/reduce_sum | solution.py:112
  241.8 0.9 multiply_reduce_fusion.8
  244.1 30.4 %all-reduce = (f32[64,64]{0,1:T(8,128)S(1)}, f32[64,64]{0,1:T(8,128)S(1)}) all-reduce(f32[64,64]{0,1:T(8,128)} %get-tuple-element.237, f32[64,64]{0,1:T(8,128)} %get-tuple-element.238), channel_id=1, replica_groups=mesh['parts'=2,'src'=8,'tile'=2] {'src'}, use_global_device_ids=true, to_apply=%region_16.17 | all-reduce | flops 8192 | bytes 65536 | tf_op jit(solution)/shard_map/psum | solution.py:187
  274.5 1.3 fusion.68
  275.8 1.6 fusion.69
  277.5 8.8 %collective-permute-start.2 = (f32[64,512]{1,0:T(8,128)S(1)}, f32[64,512]{1,0:T(8,128)S(1)}, u32[]{:S(2)}, u32[]{:S(2)}) collective-permute-start(f32[64,512]{1,0:T(8,128)S(1)} %slice_select_fusion), channel_id=1, source_target_pairs={{0,1},{1,0},{2,3},{3,2},{4,5},{5,4},{6,7},{7,6},{8,9},{9,8},{10,11... | collective-permute-start | bytes 393224 | tf_op jit(solution)/shard_map/ppermute | solution.py:39
  286.3 2.5 psum.31
  (204 shorter events, 37.5 us)
Async XLA Ops:
  7.2 7.3 %copy-start.11 = (bf16[512,512]{1,0:T(8,128)(2,1)S(1)}, bf16[512,512]{1,0:T(8,128)(2,1)}, u32[]{:S(2)}) copy-start(bf16[512,512]{1,0:T(8,128)(2,1)} %param.11) | copy-start | bytes 1572868
  7.2 130.5 %all-reduce.3.cloned.1.call-start = ((), (), s32[]{:S(2)}) async-start(), calls=%async_computation | async-start | bytes 1048576 | tf_op jit(solution)/shard_map/psum | solution.py:167
  8.2 6.3 %collective-permute-start.1 = (bf16[64,512]{1,0:T(8,128)(2,1)S(1)}, bf16[64,512]{1,0:T(8,128)(2,1)S(1)}, u32[]{:S(2)}, u32[]{:S(2)}) collective-permute-start(bf16[64,512]{1,0:T(8,128)(2,1)S(1)} %get-tuple-element.481), channel_id=1, source_target_pairs={{1,0},{3,2},{5,4},{7,6},{9,8},{11,10},{13,12},{15,14},{17,16},{19,... | collective-permute-start | bytes 196616 | tf_op jit(solution)/shard_map/ppermute | solution.py:29
  10.1 4.3 %collective-permute-start = (bf16[64,512]{1,0:T(8,128)(2,1)S(1)}, bf16[64,512]{1,0:T(8,128)(2,1)S(1)}, u32[]{:S(2)}, u32[]{:S(2)}) collective-permute-start(bf16[64,512]{1,0:T(8,128)(2,1)S(1)} %get-tuple-element.480), channel_id=1, source_target_pairs={{0,1},{2,3},{4,5},{6,7},{8,9},{10,11},{12,13},{14,15},{16,17},{18,... | collective-permute-start | bytes 196616 | tf_op jit(solution)/shard_map/ppermute | solution.py:27
  12.2 2.7 copy-start.5
  12.2 2.7 copy-start.6
  14.1 1.1 copy-start.7
  14.1 1.1 copy-start.8
  14.1 1.1 copy-start.9
  14.2 1.1 copy-start.10
  14.2 1.1 copy-start.12
  14.2 1.1 copy-start.13
  62.9 76.0 %copy-start.1 = (bf16[1024,128]{1,0:T(8,128)(2,1)}, bf16[1024,128]{1,0:T(8,128)(2,1)S(1)}, u32[]{:S(2)}) copy-start(bf16[1024,128]{1,0:T(8,128)(2,1)S(1)} %get-tuple-element.812) | copy-start | bytes 786436
  62.9 74.8 %copy-start.4 = (f32[512,512]{1,0:T(8,128)S(1)}, f32[512,512]{1,0:T(8,128)}, u32[]{:S(2)}) copy-start(f32[512,512]{1,0:T(8,128)} %param.12) | copy-start | bytes 3145732
  139.2 5.1 %copy-start.14 = (s32[4]{0:T(128)}, s32[4]{0:T(128)S(1)}, u32[]{:S(2)}) copy-start(s32[4]{0:T(128)S(1)} %get-tuple-element.797) | copy-start | bytes 52 | tf_op jit(solution)/shard_map/while
  155.7 1.3 copy-start.2
  155.7 1.5 copy-start
  163.1 1.0 copy-start.16
  163.1 2.3 copy-start.15
  164.8 0.6 copy-start.17
  165.4 5.1 %copy-start.14 = (s32[4]{0:T(128)}, s32[4]{0:T(128)S(1)}, u32[]{:S(2)}) copy-start(s32[4]{0:T(128)S(1)} %get-tuple-element.797) | copy-start | bytes 52 | tf_op jit(solution)/shard_map/while
  181.9 1.3 copy-start.2
  181.9 1.5 copy-start
  189.3 1.0 copy-start.16
  189.4 2.3 copy-start.15
  191.1 0.6 copy-start.17
  191.6 5.1 %copy-start.14 = (s32[4]{0:T(128)}, s32[4]{0:T(128)S(1)}, u32[]{:S(2)}) copy-start(s32[4]{0:T(128)S(1)} %get-tuple-element.797) | copy-start | bytes 52 | tf_op jit(solution)/shard_map/while
  208.1 1.3 copy-start.2
  208.1 1.5 copy-start
  215.6 1.0 copy-start.16
  215.6 2.3 copy-start.15
  217.3 0.6 copy-start.17
  217.9 5.1 %copy-start.14 = (s32[4]{0:T(128)}, s32[4]{0:T(128)S(1)}, u32[]{:S(2)}) copy-start(s32[4]{0:T(128)S(1)} %get-tuple-element.797) | copy-start | bytes 52 | tf_op jit(solution)/shard_map/while
  234.4 1.3 copy-start.2
  234.4 1.5 copy-start
  241.8 1.0 copy-start.16
  241.8 2.3 copy-start.15
  243.5 0.6 copy-start.17
  244.1 42.2 %copy-start.18 = (f32[4]{0:T(128)S(1)}, f32[4]{0:T(128)}, u32[]{:S(2)}) copy-start(f32[4]{0:T(128)} %get-tuple-element.239) | copy-start | bytes 52
  275.8 13.5 %copy-start.3 = (bf16[512,512]{1,0:T(8,128)(2,1)S(1)}, bf16[512,512]{1,0:T(8,128)(2,1)}, u32[]{:S(2)}) copy-start(bf16[512,512]{1,0:T(8,128)(2,1)} %all-reduce.3.cloned.1.call-done) | copy-start | bytes 1572868
  277.5 12.7 %collective-permute-start.2 = (f32[64,512]{1,0:T(8,128)S(1)}, f32[64,512]{1,0:T(8,128)S(1)}, u32[]{:S(2)}, u32[]{:S(2)}) collective-permute-start(f32[64,512]{1,0:T(8,128)S(1)} %slice_select_fusion), channel_id=1, source_target_pairs={{0,1},{1,0},{2,3},{3,2},{4,5},{5,4},{6,7},{7,6},{8,9},{9,8},{10,11... | collective-permute-start | bytes 393224 | tf_op jit(solution)/shard_map/ppermute | solution.py:39
Sparse Core Ops, SparseCore 0:
  63.9 73.7 all-reduce.2
where the time goes:
time: 300 us; the launch traced here: 298 us
  waiting for transfers between devices  73.8 us (25%)
  other arithmetic  61.3 us (20%)
  loops' own time  37 us (12%)
  local copies, waits for them, and re-layouts  33.2 us (11%)
  matrix products  33.1 us (11%)
  blocking collectives  32.8 us (11%)
  between operations  14.4 us (5%)
  starting transfers between devices  12.1 us (4%)
    psum x1, waiting for transfers between devices, body(): lax.psum(partial_image.astype(jnp.bfloat16), 'src').astype(jnp.float32)  73.8 us
    psum x1, blocking collectives, body(): total_re, total_im = lax.psum((grad_re, grad_im), 'src')  30.4 us
    dot_general x8, matrix products, field_of(): jnp.einsum('cpk,kq->cpq', row_field, col_inv, preferred_element_type=jnp....  22.6 us
    another operation x1, loops' own time, body(): lax.scan(backward, (empty, empty), (source_weights, pupil_offsets, polar_...  18.6 us
    another operation x1, loops' own time, body(): lax.scan(forward, jnp.zeros((TH, TW), jnp.float32), (source_weights, pupi...  18.4 us
    reduce_sum x8, other arithmetic, intensity_of(): jnp.sum(field[..., :TW] * field[..., :TW] + field[..., TW:] * field[...,...  18.4 us
    reduce_sum x8, other arithmetic, pupil_of(): pupil_re = jnp.sum(window[0] * vec_re - window[1] * vec_im, 1)  12.6 us
    dynamic_slice x24, local copies, waits for them, and re-layouts, body(): lax.scan(forward, jnp.zeros((TH, TW), jnp.float32), (source_weights, pupi...  9.97 us
  transfers between devices with their start and end apart: 4, of which 1 were waited for; matrix products, arithmetic and copies ran while one was open for 1% of the time, Pallas kernels for 0%

commit v1 on v0

v1 whole, which is shorter than its diff:
```python
import functools
import math

import jax
import jax.numpy as jnp
import ml_dtypes
import numpy as np
from jax import lax
from jax.experimental import pallas as pl
from jax.experimental.pallas import tpu as pltpu
from jax.sharding import PartitionSpec as P

AMB = 64
K = 64
GRAD_SCALE = 32.0
LANES = 2 * K
ROWS_16 = 16


def split_bf16(table):
    high = table.astype(ml_dtypes.bfloat16)
    low = (table - high.astype(np.float64)).astype(ml_dtypes.bfloat16)
    return high, low


def tables(th, tw):
    window = th + 2 * AMB
    grid = 2 * K
    orders = np.arange(K) - K // 2
    diffs = np.arange(-(K - 1), K)

    def angle(left, right, period):
        return 2.0 * np.pi * np.mod(np.outer(left, right), period) / period

    bf = lambda x: np.ascontiguousarray(x).astype(ml_dtypes.bfloat16)
    col = angle(np.arange(tw), orders, tw)
    col_fwd = np.concatenate([np.cos(col), -np.sin(col)], 1)
    row = angle(orders, np.arange(window), window)
    row_fwd = np.concatenate([np.cos(row), np.sin(row)], 0)
    row_amb = np.stack([row_fwd[:, th + AMB :], row_fwd[:, :AMB]])
    row_back = row_fwd[:, AMB : AMB + th].T
    amb_back = np.zeros((2, th, 2 * K))
    amb_back[0, th - AMB :] = row_fwd[:, :AMB].T
    amb_back[1, :AMB] = row_fwd[:, th + AMB :].T
    small = angle(np.arange(grid), orders, grid)
    cos, sin = np.cos(small), np.sin(small)
    row_inv = np.concatenate(
        [np.concatenate([cos, -sin], 1), np.concatenate([sin, cos], 1)], 0
    )
    col_inv = np.concatenate(
        [np.concatenate([cos.T, sin.T], 1), np.concatenate([-sin.T, cos.T], 1)], 0
    )
    back = col_inv.T
    col_back = np.concatenate([back, back[:, K:], -back[:, :K]], 1)

    def dirichlet(positions):
        turn = positions[:, None] - np.arange(grid)[None, :] / grid
        return np.cos(2.0 * np.pi * turn[:, :, None] * diffs).sum(-1) / grid

    d_row = dirichlet((np.arange(th) + AMB) / window)
    d_col = dirichlet(np.arange(tw) / tw)
    gram = (tw / grid) * (d_row.T @ d_row)
    return dict(
        col_fwd=bf(col_fwd),
        row_fwd=bf(row_fwd[:, AMB : AMB + th]),
        row_amb=bf(row_amb),
        d_col_t=bf(d_col),
        d_row_t=bf(d_row.T),
        col_inv=bf(col_inv / K),
        row_inv=bf(row_inv),
        gram=np.concatenate(split_bf16(gram), 1),
        row_inv_t=bf(row_inv.T),
        col_back=bf(col_back),
        d_col=bf(np.concatenate([d_col.T, d_col.T], 0)),
        col_fwd_t=bf(col_fwd.T),
        d_row=np.concatenate(split_bf16(d_row), 1),
        row_back=bf(row_back),
        amb_back=bf(amb_back),
    )


OWN_ROWS = ("d_row", "row_back", "amb_back")


def dot(a, b):
    return jnp.dot(a, b, preferred_element_type=jnp.float32)


def kernel(names, sizes, *refs):
    n, local, th, tw, share, owners, block_rows, edges, parts_total = sizes
    grid = 2 * K
    count = len(names)
    offsets, ids, weights, polar = refs[:4]
    hbm = dict(zip(names, refs[4 : 4 + count]))
    image_out, grad_out, source_out = refs[4 + count : 7 + count]
    vmem = dict(zip(names, refs[7 + count : 7 + 2 * count]))
    (
        partial, halo, pupil_a, pupil_b, field, power, target_small,
        part, landed, reduced, whole, spec_send, spec_land, edge_land, sums, sums_land,
        load_sem, halo_sem, scatter_send, scatter_recv, gather_send, gather_recv,
        spec_ssem, spec_rsem, edge_ssem, edge_rsem, sums_sem,
    ) = refs[7 + 2 * count :]
    me = lax.axis_index("src")
    tile = lax.axis_index("tile")
    other = 1 - tile

    barrier = pltpu.get_barrier_semaphore()
    for step in range(n):
        peer = lax.rem(me + step, n)
        if step:
            pl.semaphore_signal(barrier, inc=1, device_id={"src": peer, "tile": tile})
        pl.semaphore_signal(barrier, inc=1, device_id={"src": peer, "tile": other})

    own = pl.ds(pl.multiple_of(me * share, share), share)
    loads = {}
    for i, name in enumerate(names):
        source = hbm[name]
        if name == "amb_back":
            source = source.at[tile, own]
        elif name == "row_amb":
            source = source.at[tile]
        elif name in OWN_ROWS:
            source = source.at[own]
        loads[name] = pltpu.make_async_copy(source, vmem[name], load_sem.at[i])
        loads[name].start()

    def table(name):
        loads[name].wait()
        return vmem[name][...]

    partial[...] = dot(table("mask"), table("col_fwd")).astype(jnp.bfloat16)
    pl.semaphore_wait(barrier, 2 * n - 1)
    rim = pl.ds(pl.multiple_of(other * (th - AMB), ROWS_16), AMB)
    halo_copy = pltpu.make_async_remote_copy(
        src_ref=partial.at[rim], dst_ref=halo, send_sem=halo_sem.at[0], recv_sem=halo_sem.at[1],
        device_id={"tile": other},
    )
    halo_copy.start()
    product = dot(table("row_fwd"), partial[...])

    loads["jones"].wait()
    jones = vmem["jones"]
    lane = lax.broadcasted_iota(jnp.int32, (K, LANES), 1)
    left = lane < K
    for s in range(local):
        first, second, state = offsets[s, 0], offsets[s, 1], ids[s]
        low = lax.rem(LANES - second, LANES)
        high = K - second
        vec = [[polar[state, c, i] for i in range(2)] for c in range(2)]
        for j in range(3):
            win = [
                [jones[(c * 3 + j) * 2 + i, pl.ds(first, K), :] for i in range(2)]
                for c in range(2)
            ]
            real = sum(win[0][i] * vec[0][i] - win[1][i] * vec[1][i] for i in range(2))
            imag = sum(win[0][i] * vec[1][i] + win[1][i] * vec[0][i] for i in range(2))
            rows = slice((s * 3 + j) * K, (s * 3 + j + 1) * K)
            for value, kept in ((real, pupil_a), (imag, pupil_b)):
                kept[rows] = jnp.where(
                    left, pltpu.roll(value, low, 1), pltpu.roll(value, high, 1)
                )

    projected = dot(table("target").astype(jnp.bfloat16), table("d_col_t")).astype(jnp.bfloat16)
    target_small[...] = dot(table("d_row_t"), projected)

    halo_copy.wait()
    product = product + dot(table("row_amb"), halo[...])
    sign = jnp.where(left, 1.0, -1.0)
    norm = 1.0 / math.sqrt((th + 2 * AMB) * tw)
    spec = norm * (product[:K] + sign * pltpu.roll(product[K:], K, 1))
    turned = -sign * pltpu.roll(spec, K, 1)

    col_inv = table("col_inv")
    row_inv = table("row_inv")
    total = jnp.zeros((grid, grid), jnp.float32)
    for s in range(local):
        masked = [
            pupil_a[q * K : (q + 1) * K] * spec + pupil_b[q * K : (q + 1) * K] * turned
            for q in range(3 * s, 3 * s + 3)
        ]
        cols = dot(jnp.concatenate(masked, 0).astype(jnp.bfloat16), col_inv).astype(jnp.bfloat16)
        mixed = jnp.concatenate(
            [
                jnp.concatenate([cols[j * K : (j + 1) * K, :grid], cols[j * K : (j + 1) * K, grid:]], 0)
                for j in range(3)
            ],
            1,
        )
        values = dot(row_inv, mixed)
        field[s] = values
        squares = values[:grid] * values[:grid] + values[grid:] * values[grid:]
        power_s = squares[:, :grid] + squares[:, grid : 2 * grid] + squares[:, 2 * grid :]
        power[s] = power_s
        total = total + (weights[s] / parts_total) * power_s
    part[...] = total.astype(jnp.bfloat16)

    def block(index):
        return pl.ds(pl.multiple_of(index * block_rows, block_rows), block_rows)

    def guarded(condition, run):
        if owners == n:
            run()
        else:
            pl.when(condition)(run)

    scatter, gather = {}, {}
    for step in range(1, n):
        peer = lax.rem(me + step, n)
        to = peer if owners == n else jnp.minimum(peer, owners - 1)
        scatter[step] = pltpu.make_async_remote_copy(
            src_ref=part.at[block(to)], dst_ref=landed.at[step],
            send_sem=scatter_send.at[step], recv_sem=scatter_recv.at[step],
            device_id={"src": peer},
        )
        guarded(peer < owners, scatter[step].start)
    mine = me if owners == n else jnp.minimum(me, owners - 1)

    def reduce_own():
        acc = part[block(mine), :].astype(jnp.float32)
        for step in range(1, n):
            scatter[step].wait_recv()
            acc = acc + landed[step].astype(jnp.float32)
        reduced[...] = acc.astype(jnp.bfloat16)
        for step in range(1, n):
            gather[step].start()
        whole[block(mine), :] = reduced[...]

    for step in range(1, n):
        peer = lax.rem(me + step, n)
        gather[step] = pltpu.make_async_remote_copy(
            src_ref=reduced, dst_ref=whole.at[block(mine)],
            send_sem=gather_send.at[step], recv_sem=gather_recv.at[step],
            device_id={"src": peer},
        )
    guarded(me < owners, reduce_own)
    row_inv_t = table("row_inv_t")
    col_back = table("col_back")
    gram = table("gram")
    for step in range(1, n):
        origin = lax.rem(me + n - step, n)
        guarded(origin < owners, gather[step].wait_recv)

    image = whole[...]
    twice = jnp.concatenate([image, image], 0)
    residual = dot(gram, twice) - target_small[...]
    doubled = jnp.concatenate([residual, residual], 0)

    grad = jnp.zeros((K, LANES), jnp.float32)
    scale = 2.0 / (parts_total * K)
    for s in range(local):
        values = field[s]
        scaled = jnp.concatenate(
            [doubled * values[:, j * grid : (j + 1) * grid] for j in range(3)], 1
        ).astype(jnp.bfloat16)
        rows = dot(row_inv_t, scaled).astype(jnp.bfloat16)
        mixed = jnp.concatenate(
            [
                jnp.concatenate(
                    [rows[:K, j * grid : (j + 1) * grid], rows[K:, j * grid : (j + 1) * grid]], 1
                )
                for j in range(3)
            ],
            0,
        )
        both = dot(mixed, col_back)
        own_grad = jnp.zeros((K, LANES), jnp.float32)
        for j in range(3):
            q = 3 * s + j
            rows_q = slice(q * K, (q + 1) * K)
            pair = both[j * K : (j + 1) * K]
            own_grad = own_grad + pupil_a[rows_q] * pair[:, :LANES] + pupil_b[rows_q] * pair[:, LANES:]
        grad = grad + (scale * weights[s]) * own_grad
    spec_send[...] = (norm * grad).astype(jnp.bfloat16)

    spread, rims = {}, []
    for step in range(1, n):
        peer = lax.rem(me + step, n)
        spread[step] = pltpu.make_async_remote_copy(
            src_ref=spec_send, dst_ref=spec_land.at[step],
            send_sem=spec_ssem.at[step], recv_sem=spec_rsem.at[step],
            device_id={"src": peer},
        )
        spread[step].start()
    for e in range(edges):
        rims.append(
            pltpu.make_async_remote_copy(
                src_ref=spec_send, dst_ref=edge_land.at[me],
                send_sem=edge_ssem.at[e], recv_sem=edge_rsem.at[me],
                device_id={"src": e + tile * (n - edges), "tile": other},
            )
        )
        rims[-1].start()
    for s in range(local):
        sums[s : s + 1, :] = jnp.sum(residual * power[s], 0, keepdims=True)
    sums_copy = pltpu.make_async_remote_copy(
        src_ref=sums, dst_ref=sums_land, send_sem=sums_sem.at[0], recv_sem=sums_sem.at[1],
        device_id={"tile": other},
    )
    sums_copy.start()

    lines = dot(table("d_row"), twice)
    lines_high = lines.astype(jnp.bfloat16)
    lines_low = (lines - lines_high.astype(jnp.float32)).astype(jnp.bfloat16)
    image_out[0] = dot(jnp.concatenate([lines_high, lines_low], 1), table("d_col"))

    row_back, amb_back, col_fwd_t = table("row_back"), table("amb_back"), table("col_fwd_t")
    sums_copy.wait()
    both_sums = sums[...] + sums_land[...]
    for s in range(local):
        source_out[s] = jnp.sum(both_sums[s : s + 1, :]) / (2 * th * tw)

    def stack(value):
        return jnp.concatenate([value, -sign * pltpu.roll(value, K, 1)], 0).astype(jnp.bfloat16)

    summed = spec_send[...].astype(jnp.float32)
    for step in range(1, n):
        spread[step].wait_recv()
        summed = summed + spec_land[step].astype(jnp.float32)
    rows = dot(row_back, stack(summed))
    at_rim = jnp.where(tile == 0, me >= n - edges, me < edges)

    @pl.when(at_rim)
    def _():
        outer = jnp.zeros((K, LANES), jnp.float32)
        for d in range(n):
            pltpu.make_async_remote_copy(
                src_ref=spec_send, dst_ref=edge_land.at[d],
                send_sem=edge_ssem.at[0], recv_sem=edge_rsem.at[d],
                device_id={"tile": other},
            ).wait_recv()
            outer = outer + edge_land[d].astype(jnp.float32)
        full = rows + dot(amb_back, stack(outer))
        grad_out[0] = GRAD_SCALE * dot(full.astype(jnp.bfloat16), col_fwd_t)

    @pl.when(jnp.logical_not(at_rim))
    def _():
        grad_out[0] = GRAD_SCALE * dot(rows.astype(jnp.bfloat16), col_fwd_t)

    for step in range(1, n):
        guarded(lax.rem(me + step, n) < owners, scatter[step].wait_send)
        guarded(me < owners, gather[step].wait_send)
        spread[step].wait_send()
    for copy in rims:
        copy.wait_send()


def body(
    mask_values, target_image, jones_pupil, polar_states, source_weights, pupil_offsets, polar_ids
):
    th, tw = mask_values.shape
    n = lax.axis_size("src")
    assert lax.axis_size("tile") == 2
    local = source_weights.shape[0]
    share = th // n
    grid = 2 * K
    owners = min(n, grid // ROWS_16)
    block_rows = grid // owners
    assert owners * block_rows == grid
    edges = -(-AMB // share)
    named = dict(
        mask=mask_values,
        target=target_image,
        jones=jones_pupil.reshape((-1,) + jones_pupil.shape[-2:]),
    )
    constants = tables(th, tw)
    order = ["mask", "col_fwd", "row_fwd", "jones", "target", "d_col_t", "d_row_t"]
    order += [name for name in constants if name not in order]
    arrays = []
    held = []
    for name in order:
        value = named[name] if name in named else jnp.asarray(constants[name])
        arrays.append(value)
        shape = value.shape
        if name == "amb_back":
            shape = (share,) + shape[2:]
        elif name == "row_amb":
            shape = shape[1:]
        elif name in OWN_ROWS:
            shape = (share,) + shape[1:]
        held.append(pltpu.VMEM(shape, value.dtype))
    f32, bf16 = jnp.float32, jnp.bfloat16
    sems = pltpu.SemaphoreType.DMA
    scratch = held + [
        pltpu.VMEM((th, LANES), bf16),
        pltpu.VMEM((AMB, LANES), bf16),
        pltpu.VMEM((3 * local * K, LANES), f32),
        pltpu.VMEM((3 * local * K, LANES), f32),
        pltpu.VMEM((local, 2 * grid, 3 * grid), f32),
        pltpu.VMEM((local, grid, grid), f32),
        pltpu.VMEM((grid, grid), f32),
        pltpu.VMEM((grid, grid), bf16),
        pltpu.VMEM((n, block_rows, grid), bf16),
        pltpu.VMEM((block_rows, grid), bf16),
        pltpu.VMEM((grid, grid), bf16),
        pltpu.VMEM((K, LANES), bf16),
        pltpu.VMEM((n, K, LANES), bf16),
        pltpu.VMEM((n, K, LANES), bf16),
        pltpu.VMEM((local, LANES), f32),
        pltpu.VMEM((local, LANES), f32),
        sems((len(order),)),
        sems((2,)),
        sems((n,)),
        sems((n,)),
        sems((n,)),
        sems((n,)),
        sems((n,)),
        sems((n,)),
        sems((edges,)),
        sems((n,)),
        sems((2,)),
    ]
    sizes = (n, local, th, tw, share, owners, block_rows, edges, local * n)
    smem = pl.BlockSpec(memory_space=pltpu.SMEM)
    return pl.pallas_call(
        functools.partial(kernel, tuple(order), sizes),
        out_shape=(
            jax.ShapeDtypeStruct((1, share, tw), f32),
            jax.ShapeDtypeStruct((1, share, tw), f32),
            jax.ShapeDtypeStruct((local,), f32),
        ),
        in_specs=[smem] * 4 + [pl.BlockSpec(memory_space=pl.ANY)] * len(arrays),
        out_specs=(
            pl.BlockSpec(memory_space=pltpu.VMEM),
            pl.BlockSpec(memory_space=pltpu.VMEM),
            smem,
        ),
        scratch_shapes=scratch,
        compiler_params=pltpu.CompilerParams(
            collective_id=0, has_side_effects=True, vmem_limit_bytes=48 * 1024 * 1024
        ),
    )(pupil_offsets, polar_ids, source_weights, polar_states, *arrays)


def solution(mesh):
    placed = (
        P(("parts", "tile"), None),
        P(("parts", "tile"), None),
        P(),
        P(),
        P(("parts", "src")),
        P(("parts", "src"), None),
        P(("parts", "src")),
    )
    return jax.shard_map(
        body,
        mesh=mesh,
        in_specs=placed,
        out_specs=(
            P(("parts", "tile"), "src", None),
            P(("parts", "tile"), "src", None),
            P(("parts", "src")),
        ),
        check_vma=False,
    )
```

time: 300 us -> 46 us (0.15)
  waiting for transfers between devices: 73.8 us -> 0 us
  other arithmetic: 61.3 us -> 0 us
  loops' own time: 37 us -> 0 us
  matrix products: 33.1 us -> 0 us
  blocking collectives: 32.8 us -> 0 us
  Pallas kernels: 0 us -> 24.5 us
  between operations: 14.4 us -> 0.68 us
  local copies, waits for them, and re-layouts: 33.2 us -> 20 us
  starting transfers between devices: 12.1 us -> 0 us
    psum x1 -> x0, waiting for transfers between devices: 73.8 us -> none  [body(): lax.psum(partial_image.astype(jnp.bfloat16), 'src').astype(jnp.float32)]
    reduce_sum x32 -> x0, other arithmetic: 38.3 us -> none  [the longest x8 18.4 us: intensity_of(): jnp.sum(field[..., :TW] * field[..., :TW] + field[..., TW:] * field[...,...]
    another operation x2 -> x0, loops' own time: 37 us -> none  [the longest x1 18.6 us: body(): lax.scan(backward, (empty, empty), (source_weights, pupil_offsets, polar_...]
    dot_general x23 -> x0, matrix products: 33.1 us -> none  [the longest x8 22.6 us: field_of(): jnp.einsum('cpk,kq->cpq', row_field, col_inv, preferred_element_type=jnp....]
    psum x2 -> x0, blocking collectives: 32.8 us -> none  [the longest x1 30.4 us: body(): total_re, total_im = lax.psum((grad_re, grad_im), 'src')]
    pallas_call x0 -> x1, Pallas kernels: none -> 24.5 us  [body(): pl.pallas_call(functools.partial(kernel, tuple(order), sizes), out_shape=...]
    unnamed x29 -> x49, local copies, waits for them, and re-layouts: 0.39 us -> 20 us
    ppermute x3 -> x0, starting transfers between devices: 12.1 us -> none  [the longest x1 8.8 us: partner(): return lax.ppermute(value, axis, pairs)]
  transfers between devices with their start and end apart: 4 -> 0, of which waited for: 1 -> 0; matrix products, arithmetic and copies ran while one was open for 1% -> 0% of each run, Pallas kernels for 0% -> 0%
where the time goes in v1:
time: 46 us; the launch traced here: 45.2 us
  Pallas kernels  24.5 us (53%)
  local copies, waits for them, and re-layouts  20 us (43%)
  between operations  0.68 us (1%)
    pallas_call x1, Pallas kernels, body(): pl.pallas_call(functools.partial(kernel, tuple(order), sizes), out_shape=...  24.5 us
    unnamed x49, local copies, waits for them, and re-layouts  20 us

profile of v1, /device:TPU:1, one launch (start us, length us, event | category | flops | bytes accessed | tf_op | source)
XLA Modules:
  0.0 45.2 jit_solution(9333269343485897995)
XLA Ops:
  0.6 0.0 copy-start.21
  0.6 0.0 copy-start.20
  0.7 0.7 %copy-done.21 = s32[4,2]{0,1:T(2,128)S(1)} copy-done((s32[4,2]{0,1:T(2,128)S(1)}, s32[4,2]{0,1:T(2,128)}, u32[]{:S(2)}) %copy-start.21) | copy-done | bytes 56
  1.3 0.1 copy.25.refs_0_
  1.4 0.0 copy-done.20
  1.4 0.0 copy-start.18
  1.4 0.0 copy-start.19
  1.4 0.1 copy.26.refs_3_
  1.5 0.6 %copy-done.18 = s32[4]{0:T(128)S(1)} copy-done((s32[4]{0:T(128)S(1)}, s32[4]{0:T(128)}, u32[]{:S(2)}) %copy-start.18) | copy-done | bytes 40
  2.1 0.0 copy-done.19
  2.1 0.0 copy-start
  2.1 1.2 %copy-done = f32[512,512]{1,0:T(8,128)S(1)} copy-done((f32[512,512]{1,0:T(8,128)S(1)}, f32[512,512]{1,0:T(8,128)}, u32[]{:S(2)}) %copy-start) | copy-done | bytes 1048600
  3.3 0.0 copy-start.1
  3.3 1.1 %copy-done.1 = f32[2,3,2,128,128]{4,3,2,1,0:T(8,128)S(1)} copy-done((f32[2,3,2,128,128]{4,3,2,1,0:T(8,128)S(1)}, f32[2,3,2,128,128]{4,3,2,1,0:T(8,128)}, u32[]{:S(2)}) %copy-start.1) | copy-done | bytes 786456
  4.4 0.0 copy-start.2
  4.4 1.0 %copy-done.2 = bf16[512,512]{1,0:T(8,128)(2,1)S(1)} copy-done((bf16[512,512]{1,0:T(8,128)(2,1)S(1)}, bf16[512,512]{1,0:T(8,128)(2,1)}, u32[]{:S(2)}) %copy-start.2) | copy-done | bytes 524312
  5.5 0.0 copy-start.3
  5.5 0.9 %copy-done.3 = bf16[2,512,128]{2,1,0:T(8,128)(2,1)S(1)} copy-done((bf16[2,512,128]{2,1,0:T(8,128)(2,1)S(1)}, bf16[2,512,128]{2,1,0:T(8,128)(2,1)}, u32[]{:S(2)}) %copy-start.3) | copy-done | bytes 262168
  6.4 0.0 copy-start.4
  6.4 0.9 %copy-done.4 = bf16[512,256]{1,0:T(8,128)(2,1)S(1)} copy-done((bf16[512,256]{1,0:T(8,128)(2,1)S(1)}, bf16[512,256]{1,0:T(8,128)(2,1)}, u32[]{:S(2)}) %copy-start.4) | copy-done | bytes 262168
  7.4 0.0 copy-start.5
  7.4 0.9 %copy-done.5 = bf16[256,512]{1,0:T(8,128)(2,1)S(1)} copy-done((bf16[256,512]{1,0:T(8,128)(2,1)S(1)}, bf16[256,512]{1,0:T(8,128)(2,1)}, u32[]{:S(2)}) %copy-start.5) | copy-done | bytes 262168
  8.3 0.0 copy-start.6
  8.3 0.9 %copy-done.6 = bf16[512,128]{1,0:T(8,128)(2,1)S(1)} copy-done((bf16[512,128]{1,0:T(8,128)(2,1)S(1)}, bf16[512,128]{1,0:T(8,128)(2,1)}, u32[]{:S(2)}) %copy-start.6) | copy-done | bytes 131096
  9.2 0.0 copy-start.7
  9.2 0.9 %copy-done.7 = bf16[128,512]{1,0:T(8,128)(2,1)S(1)} copy-done((bf16[128,512]{1,0:T(8,128)(2,1)S(1)}, bf16[128,512]{1,0:T(8,128)(2,1)}, u32[]{:S(2)}) %copy-start.7) | copy-done | bytes 131096
  10.1 0.0 copy-start.8
  10.1 0.9 %copy-done.8 = bf16[256,256]{1,0:T(8,128)(2,1)S(1)} copy-done((bf16[256,256]{1,0:T(8,128)(2,1)S(1)}, bf16[256,256]{1,0:T(8,128)(2,1)}, u32[]{:S(2)}) %copy-start.8) | copy-done | bytes 131096
  11.0 0.0 copy-start.9
  11.0 0.9 %copy-done.9 = bf16[128,512]{1,0:T(8,128)(2,1)S(1)} copy-done((bf16[128,512]{1,0:T(8,128)(2,1)S(1)}, bf16[128,512]{1,0:T(8,128)(2,1)}, u32[]{:S(2)}) %copy-start.9) | copy-done | bytes 131096
  11.9 0.0 copy-start.10
  12.0 0.9 %copy-done.10 = bf16[512,128]{1,0:T(8,128)(2,1)S(1)} copy-done((bf16[512,128]{1,0:T(8,128)(2,1)S(1)}, bf16[512,128]{1,0:T(8,128)(2,1)}, u32[]{:S(2)}) %copy-start.10) | copy-done | bytes 131096
  12.9 0.0 copy-start.11
  12.9 0.9 %copy-done.11 = bf16[128,512]{1,0:T(8,128)(2,1)S(1)} copy-done((bf16[128,512]{1,0:T(8,128)(2,1)S(1)}, bf16[128,512]{1,0:T(8,128)(2,1)}, u32[]{:S(2)}) %copy-start.11) | copy-done | bytes 131096
  13.8 0.0 copy-start.12
  13.8 0.9 %copy-done.12 = bf16[512,128]{1,0:T(8,128)(2,1)S(1)} copy-done((bf16[512,128]{1,0:T(8,128)(2,1)S(1)}, bf16[512,128]{1,0:T(8,128)(2,1)}, u32[]{:S(2)}) %copy-start.12) | copy-done | bytes 131096
  14.7 0.0 copy-start.13
  14.7 0.8 %copy-done.13 = bf16[128,256]{1,0:T(8,128)(2,1)S(1)} copy-done((bf16[128,256]{1,0:T(8,128)(2,1)S(1)}, bf16[128,256]{1,0:T(8,128)(2,1)}, u32[]{:S(2)}) %copy-start.13) | copy-done | bytes 65560
  15.5 0.0 copy-start.14
  15.5 0.8 %copy-done.14 = bf16[128,256]{1,0:T(8,128)(2,1)S(1)} copy-done((bf16[128,256]{1,0:T(8,128)(2,1)S(1)}, bf16[128,256]{1,0:T(8,128)(2,1)}, u32[]{:S(2)}) %copy-start.14) | copy-done | bytes 65560
  16.3 0.0 copy-start.15
  16.3 0.8 %copy-done.15 = bf16[256,128]{1,0:T(8,128)(2,1)S(1)} copy-done((bf16[256,128]{1,0:T(8,128)(2,1)S(1)}, bf16[256,128]{1,0:T(8,128)(2,1)}, u32[]{:S(2)}) %copy-start.15) | copy-done | bytes 65560
  17.2 0.0 copy-start.16
  17.2 0.8 %copy-done.16 = bf16[128,256]{1,0:T(8,128)(2,1)S(1)} copy-done((bf16[128,256]{1,0:T(8,128)(2,1)S(1)}, bf16[128,256]{1,0:T(8,128)(2,1)}, u32[]{:S(2)}) %copy-start.16) | copy-done | bytes 65560
  18.0 0.0 copy-start.17
  18.0 0.8 %copy-done.17 = bf16[2,128,64]{2,1,0:T(8,128)(2,1)S(1)} copy-done((bf16[2,128,64]{2,1,0:T(8,128)(2,1)S(1)}, bf16[2,128,64]{2,1,0:T(8,128)(2,1)}, u32[]{:S(2)}) %copy-start.17) | copy-done | bytes 32792
  18.9 24.5 %shard_map.229 = (f32[1,64,512]{2,1,0:T(8,128)S(1)}, f32[1,64,512]{2,1,0:T(8,128)S(1)}, f32[4]{0:T(128)S(1)}) custom-call(s32[4,2]{1,0:T(4,128)S(1)} %copy.25.refs_0_, s32[4]{0:T(128)S(1)} %copy-done.18, f32[4]{0:T(128)S(1)} %copy-done.19, f32[4,2,2]{2,1,0:T(2,128)S(1)} %copy.26.refs_3_, bf16[512,512]{1,0:T(8,128)(2,1)S(1)} %copy-done.2, ...), custom_call_target="tpu_custom_call" | custom-call | tf_op jit(solution)/shard_map/pallas_call | solution.py:414
  43.4 0.7 %copy.30 = f32[1,64,512]{2,1,0:T(8,128)} copy(f32[1,64,512]{2,1,0:T(8,128)S(1)} %get-tuple-element.6) | data formatting | bytes 262144
  44.1 0.7 %copy.31 = f32[1,64,512]{2,1,0:T(8,128)} copy(f32[1,64,512]{2,1,0:T(8,128)S(1)} %get-tuple-element.7) | data formatting | bytes 262144
  44.7 0.5 %copy.32 = f32[4]{0:T(128)} copy(f32[4]{0:T(128)S(1)} %get-tuple-element.8) | data formatting | bytes 32
Async XLA Ops:
  0.6 0.7 %copy-start.21 = (s32[4,2]{0,1:T(2,128)S(1)}, s32[4,2]{0,1:T(2,128)}, u32[]{:S(2)}) copy-start(s32[4,2]{0,1:T(2,128)} %param.27) | copy-start | bytes 100
  0.6 0.8 %copy-start.20 = (f32[4,2,2]{0,2,1:T(2,128)S(1)}, f32[4,2,2]{0,2,1:T(2,128)}, u32[]{:S(2)}) copy-start(f32[4,2,2]{0,2,1:T(2,128)} %param.25) | copy-start | bytes 196
  1.4 0.7 %copy-start.18 = (s32[4]{0:T(128)S(1)}, s32[4]{0:T(128)}, u32[]{:S(2)}) copy-start(s32[4]{0:T(128)} %refs_1_.1) | copy-start | bytes 52
  1.4 0.7 %copy-start.19 = (f32[4]{0:T(128)S(1)}, f32[4]{0:T(128)}, u32[]{:S(2)}) copy-start(f32[4]{0:T(128)} %refs_2_.1) | copy-start | bytes 52
  2.1 1.2 %copy-start = (f32[512,512]{1,0:T(8,128)S(1)}, f32[512,512]{1,0:T(8,128)}, u32[]{:S(2)}) copy-start(f32[512,512]{1,0:T(8,128)} %refs_8_.1) | copy-start | bytes 3145732
  3.3 1.1 %copy-start.1 = (f32[2,3,2,128,128]{4,3,2,1,0:T(8,128)S(1)}, f32[2,3,2,128,128]{4,3,2,1,0:T(8,128)}, u32[]{:S(2)}) copy-start(f32[2,3,2,128,128]{4,3,2,1,0:T(8,128)} %param.24) | copy-start | bytes 2359300
  4.4 1.0 %copy-start.2 = (bf16[512,512]{1,0:T(8,128)(2,1)S(1)}, bf16[512,512]{1,0:T(8,128)(2,1)}, u32[]{:S(2)}) copy-start(bf16[512,512]{1,0:T(8,128)(2,1)} %refs_4_.1) | copy-start | bytes 1572868
  5.5 0.9 %copy-start.3 = (bf16[2,512,128]{2,1,0:T(8,128)(2,1)S(1)}, bf16[2,512,128]{2,1,0:T(8,128)(2,1)}, u32[]{:S(2)}) copy-start(bf16[2,512,128]{2,1,0:T(8,128)(2,1)} %constant.44.clone.refs_21_) | copy-start | bytes 786436
  6.4 0.9 %copy-start.4 = (bf16[512,256]{1,0:T(8,128)(2,1)S(1)}, bf16[512,256]{1,0:T(8,128)(2,1)}, u32[]{:S(2)}) copy-start(bf16[512,256]{1,0:T(8,128)(2,1)} %constant.42.clone.refs_19_) | copy-start | bytes 786436
  7.4 0.9 %copy-start.5 = (bf16[256,512]{1,0:T(8,128)(2,1)S(1)}, bf16[256,512]{1,0:T(8,128)(2,1)}, u32[]{:S(2)}) copy-start(bf16[256,512]{1,0:T(8,128)(2,1)} %constant.40.clone.refs_17_) | copy-start | bytes 786436
  8.3 0.9 %copy-start.6 = (bf16[512,128]{1,0:T(8,128)(2,1)S(1)}, bf16[512,128]{1,0:T(8,128)(2,1)}, u32[]{:S(2)}) copy-start(bf16[512,128]{1,0:T(8,128)(2,1)} %constant.43.clone.refs_20_) | copy-start | bytes 393220
  9.2 0.9 %copy-start.7 = (bf16[128,512]{1,0:T(8,128)(2,1)S(1)}, bf16[128,512]{1,0:T(8,128)(2,1)}, u32[]{:S(2)}) copy-start(bf16[128,512]{1,0:T(8,128)(2,1)} %constant.41.clone.refs_18_) | copy-start | bytes 393220
  10.1 0.9 %copy-start.8 = (bf16[256,256]{1,0:T(8,128)(2,1)S(1)}, bf16[256,256]{1,0:T(8,128)(2,1)}, u32[]{:S(2)}) copy-start(bf16[256,256]{1,0:T(8,128)(2,1)} %constant.39.clone.refs_16_) | copy-start | bytes 393220
  11.0 0.9 %copy-start.9 = (bf16[128,512]{1,0:T(8,128)(2,1)S(1)}, bf16[128,512]{1,0:T(8,128)(2,1)}, u32[]{:S(2)}) copy-start(bf16[128,512]{1,0:T(8,128)(2,1)} %constant.33.clone.refs_10_) | copy-start | bytes 393220
  11.9 0.9 %copy-start.10 = (bf16[512,128]{1,0:T(8,128)(2,1)S(1)}, bf16[512,128]{1,0:T(8,128)(2,1)}, u32[]{:S(2)}) copy-start(bf16[512,128]{1,0:T(8,128)(2,1)} %constant.32.clone.refs_9_) | copy-start | bytes 393220
  12.9 0.9 %copy-start.11 = (bf16[128,512]{1,0:T(8,128)(2,1)S(1)}, bf16[128,512]{1,0:T(8,128)(2,1)}, u32[]{:S(2)}) copy-start(bf16[128,512]{1,0:T(8,128)(2,1)} %constant.31.clone.refs_6_) | copy-start | bytes 393220
  13.8 0.9 %copy-start.12 = (bf16[512,128]{1,0:T(8,128)(2,1)S(1)}, bf16[512,128]{1,0:T(8,128)(2,1)}, u32[]{:S(2)}) copy-start(bf16[512,128]{1,0:T(8,128)(2,1)} %constant.30.clone.refs_5_) | copy-start | bytes 393220
  14.7 0.8 %copy-start.13 = (bf16[128,256]{1,0:T(8,128)(2,1)S(1)}, bf16[128,256]{1,0:T(8,128)(2,1)}, u32[]{:S(2)}) copy-start(bf16[128,256]{1,0:T(8,128)(2,1)} %constant.38.clone.refs_15_) | copy-start | bytes 196612
  15.5 0.8 %copy-start.14 = (bf16[128,256]{1,0:T(8,128)(2,1)S(1)}, bf16[128,256]{1,0:T(8,128)(2,1)}, u32[]{:S(2)}) copy-start(bf16[128,256]{1,0:T(8,128)(2,1)} %constant.37.clone.refs_14_) | copy-start | bytes 196612
  16.3 0.8 %copy-start.15 = (bf16[256,128]{1,0:T(8,128)(2,1)S(1)}, bf16[256,128]{1,0:T(8,128)(2,1)}, u32[]{:S(2)}) copy-start(bf16[256,128]{1,0:T(8,128)(2,1)} %constant.36.clone.refs_13_) | copy-start | bytes 196612
  17.2 0.8 %copy-start.16 = (bf16[128,256]{1,0:T(8,128)(2,1)S(1)}, bf16[128,256]{1,0:T(8,128)(2,1)}, u32[]{:S(2)}) copy-start(bf16[128,256]{1,0:T(8,128)(2,1)} %constant.35.clone.refs_12_) | copy-start | bytes 196612
  18.0 0.8 %copy-start.17 = (bf16[2,128,64]{2,1,0:T(8,128)(2,1)S(1)}, bf16[2,128,64]{2,1,0:T(8,128)(2,1)}, u32[]{:S(2)}) copy-start(bf16[2,128,64]{2,1,0:T(8,128)(2,1)} %constant.34.clone.refs_11_) | copy-start | bytes 98308

commit v2 on v1

--- a/solution.py
+++ b/solution.py
@@ -14,6 +14,7 @@
 K = 64
 GRAD_SCALE = 32.0
 LANES = 2 * K
+VMEM_LIMIT = 64 * 1024 * 1024 - 512 * 1024
 ROWS_16 = 16
 
 
@@ -79,6 +80,7 @@
     )
 
 
+SCALARS = ("offsets", "ids", "weights", "polar")
 OWN_ROWS = ("d_row", "row_back", "amb_back")
 
 
@@ -90,16 +92,17 @@
     n, local, th, tw, share, owners, block_rows, edges, parts_total = sizes
     grid = 2 * K
     count = len(names)
-    offsets, ids, weights, polar = refs[:4]
-    hbm = dict(zip(names, refs[4 : 4 + count]))
-    image_out, grad_out, source_out = refs[4 + count : 7 + count]
-    vmem = dict(zip(names, refs[7 + count : 7 + 2 * count]))
+    hbm = dict(zip(names, refs[:count]))
+    outputs = refs[count : 3 + count]
+    vmem = dict(zip(names, refs[3 + count : 3 + 2 * count]))
+    offsets, ids, weights, polar = (vmem[name] for name in SCALARS)
     (
         partial, halo, pupil_a, pupil_b, field, power, target_small,
         part, landed, reduced, whole, spec_send, spec_land, edge_land, sums, sums_land,
         load_sem, halo_sem, scatter_send, scatter_recv, gather_send, gather_recv,
         spec_ssem, spec_rsem, edge_ssem, edge_rsem, sums_sem,
-    ) = refs[7 + 2 * count :]
+        image_out, grad_out, source_out, out_sem,
+    ) = refs[3 + 2 * count :]
     me = lax.axis_index("src")
     tile = lax.axis_index("tile")
     other = 1 - tile
@@ -129,24 +132,16 @@
         return vmem[name][...]
 
     partial[...] = dot(table("mask"), table("col_fwd")).astype(jnp.bfloat16)
-    pl.semaphore_wait(barrier, 2 * n - 1)
-    rim = pl.ds(pl.multiple_of(other * (th - AMB), ROWS_16), AMB)
-    halo_copy = pltpu.make_async_remote_copy(
-        src_ref=partial.at[rim], dst_ref=halo, send_sem=halo_sem.at[0], recv_sem=halo_sem.at[1],
-        device_id={"tile": other},
-    )
-    halo_copy.start()
-    product = dot(table("row_fwd"), partial[...])
-
-    loads["jones"].wait()
+    for name in SCALARS + ("jones",):
+        loads[name].wait()
     jones = vmem["jones"]
     lane = lax.broadcasted_iota(jnp.int32, (K, LANES), 1)
     left = lane < K
     for s in range(local):
-        first, second, state = offsets[s, 0], offsets[s, 1], ids[s]
+        first, second, state = offsets[0, s], offsets[1, s], ids[s]
         low = lax.rem(LANES - second, LANES)
         high = K - second
-        vec = [[polar[state, c, i] for i in range(2)] for c in range(2)]
+        vec = [[polar[c, i, state] for i in range(2)] for c in range(2)]
         for j in range(3):
             win = [
                 [jones[(c * 3 + j) * 2 + i, pl.ds(first, K), :] for i in range(2)]
@@ -159,6 +154,15 @@
                 kept[rows] = jnp.where(
                     left, pltpu.roll(value, low, 1), pltpu.roll(value, high, 1)
                 )
+
+    pl.semaphore_wait(barrier, 2 * n - 1)
+    rim = pl.ds(pl.multiple_of(other * (th - AMB), ROWS_16), AMB)
+    halo_copy = pltpu.make_async_remote_copy(
+        src_ref=partial.at[rim], dst_ref=halo, send_sem=halo_sem.at[0], recv_sem=halo_sem.at[1],
+        device_id={"tile": other},
+    )
+    halo_copy.start()
+    product = dot(table("row_fwd"), partial[...])
 
     projected = dot(table("target").astype(jnp.bfloat16), table("d_col_t")).astype(jnp.bfloat16)
     target_small[...] = dot(table("d_row_t"), projected)
@@ -301,13 +305,20 @@
     lines = dot(table("d_row"), twice)
     lines_high = lines.astype(jnp.bfloat16)
     lines_low = (lines - lines_high.astype(jnp.float32)).astype(jnp.bfloat16)
-    image_out[0] = dot(jnp.concatenate([lines_high, lines_low], 1), table("d_col"))
+    image_out[...] = dot(jnp.concatenate([lines_high, lines_low], 1), table("d_col"))
+
+    writes = [
+        pltpu.make_async_copy(source, to, out_sem.at[i])
+        for i, (source, to) in enumerate(zip((image_out, grad_out, source_out), outputs))
+    ]
+    writes[0].start()
 
     row_back, amb_back, col_fwd_t = table("row_back"), table("amb_back"), table("col_fwd_t")
     sums_copy.wait()
-    both_sums = sums[...] + sums_land[...]
+    both_sums = jnp.sum(sums[...] + sums_land[...], 1, keepdims=True) / (2 * th * tw)
     for s in range(local):
-        source_out[s] = jnp.sum(both_sums[s : s + 1, :]) / (2 * th * tw)
+        source_out[s] = both_sums[s, 0]
+    writes[2].start()
 
     def stack(value):
         return jnp.concatenate([value, -sign * pltpu.roll(value, K, 1)], 0).astype(jnp.bfloat16)
@@ -330,18 +341,33 @@
             ).wait_recv()
             outer = outer + edge_land[d].astype(jnp.float32)
         full = rows + dot(amb_back, stack(outer))
-        grad_out[0] = GRAD_SCALE * dot(full.astype(jnp.bfloat16), col_fwd_t)
+        grad_out[...] = GRAD_SCALE * dot(full.astype(jnp.bfloat16), col_fwd_t)
 
     @pl.when(jnp.logical_not(at_rim))
     def _():
-        grad_out[0] = GRAD_SCALE * dot(rows.astype(jnp.bfloat16), col_fwd_t)
-
+        grad_out[...] = GRAD_SCALE * dot(rows.astype(jnp.bfloat16), col_fwd_t)
+
+    writes[1].start()
     for step in range(1, n):
         guarded(lax.rem(me + step, n) < owners, scatter[step].wait_send)
         guarded(me < owners, gather[step].wait_send)
         spread[step].wait_send()
     for copy in rims:
         copy.wait_send()
+    for copy in writes:
+        copy.wait()
+
+
+def write_outputs(image, grad, source, image_out, grad_out, source_out, sem):
+    copies = [
+        pltpu.make_async_copy(image, image_out.at[0], sem.at[0]),
+        pltpu.make_async_copy(grad, grad_out.at[0], sem.at[1]),
+        pltpu.make_async_copy(source, source_out, sem.at[2]),
+    ]
+    for copy in copies:
+        copy.start()
+    for copy in copies:
+        copy.wait()
 
 
 def body(
@@ -361,9 +387,13 @@
         mask=mask_values,
         target=target_image,
         jones=jones_pupil.reshape((-1,) + jones_pupil.shape[-2:]),
+        offsets=pupil_offsets.T,
+        ids=polar_ids,
+        weights=source_weights,
+        polar=polar_states.transpose(1, 2, 0),
     )
     constants = tables(th, tw)
-    order = ["mask", "col_fwd", "row_fwd", "jones", "target", "d_col_t", "d_row_t"]
+    order = ["mask", "col_fwd", *SCALARS, "jones", "row_fwd", "target", "d_col_t", "d_row_t"]
     order += [name for name in constants if name not in order]
     arrays = []
     held = []
@@ -377,7 +407,7 @@
             shape = shape[1:]
         elif name in OWN_ROWS:
             shape = (share,) + shape[1:]
-        held.append(pltpu.VMEM(shape, value.dtype))
+        held.append((pltpu.SMEM if name in SCALARS else pltpu.VMEM)(shape, value.dtype))
     f32, bf16 = jnp.float32, jnp.bfloat16
     sems = pltpu.SemaphoreType.DMA
     scratch = held + [
@@ -408,27 +438,39 @@
         sems((edges,)),
         sems((n,)),
         sems((2,)),
+        pltpu.VMEM((share, tw), f32),
+        pltpu.VMEM((share, tw), f32),
+        pltpu.SMEM((local,), f32),
+        sems((3,)),
     ]
     sizes = (n, local, th, tw, share, owners, block_rows, edges, local * n)
-    smem = pl.BlockSpec(memory_space=pltpu.SMEM)
+    in_hbm = pl.BlockSpec(memory_space=pltpu.HBM)
+    results = pl.pallas_call(
+        functools.partial(kernel, tuple(order), sizes),
+        out_shape=(
+            jax.ShapeDtypeStruct((share, tw), f32),
+            jax.ShapeDtypeStruct((share, tw), f32),
+            jax.ShapeDtypeStruct((local,), f32),
+        ),
+        in_specs=[in_hbm] * len(arrays),
+        out_specs=(in_hbm,) * 3,
+        scratch_shapes=scratch,
+        compiler_params=pltpu.CompilerParams(
+            collective_id=0, has_side_effects=True, vmem_limit_bytes=VMEM_LIMIT
+        ),
+    )(*arrays)
     return pl.pallas_call(
-        functools.partial(kernel, tuple(order), sizes),
+        write_outputs,
         out_shape=(
             jax.ShapeDtypeStruct((1, share, tw), f32),
             jax.ShapeDtypeStruct((1, share, tw), f32),
             jax.ShapeDtypeStruct((local,), f32),
         ),
-        in_specs=[smem] * 4 + [pl.BlockSpec(memory_space=pl.ANY)] * len(arrays),
-        out_specs=(
-            pl.BlockSpec(memory_space=pltpu.VMEM),
-            pl.BlockSpec(memory_space=pltpu.VMEM),
-            smem,
-        ),
-        scratch_shapes=scratch,
-        compiler_params=pltpu.CompilerParams(
-            collective_id=0, has_side_effects=True, vmem_limit_bytes=48 * 1024 * 1024
-        ),
-    )(pupil_offsets, polar_ids, source_weights, polar_states, *arrays)
+        in_specs=[in_hbm] * 3,
+        out_specs=(in_hbm,) * 3,
+        scratch_shapes=[sems((3,))],
+        compiler_params=pltpu.CompilerParams(vmem_limit_bytes=VMEM_LIMIT),
+    )(*results)
 
 
 def solution(mesh):

time: 46 us -> 33.3 us (0.72); the launches traced: 45.2 us -> 33.2 us
  local copies, waits for them, and re-layouts: 20 us -> 0 us
  Pallas kernels: 24.5 us -> 32.5 us
    unnamed x49 -> x0, local copies, waits for them, and re-layouts: 20 us -> none
    pallas_call x0 -> x1, Pallas kernels: none -> 9.09 us  [body(): pl.pallas_call(write_outputs, out_shape=(jax.ShapeDtypeStruct((1, share,...]
    pallas_call x1, Pallas kernels: 24.5 us -> 23.4 us  [body(): pl.pallas_call(functools.partial(kernel, tuple(order), sizes), out_shape=...]
where the time goes in v2:
time: 33.3 us; the launch traced here: 33.2 us
  Pallas kernels  32.5 us (98%)
  between operations  0.64 us (2%)
    pallas_call x1, Pallas kernels, body(): pl.pallas_call(functools.partial(kernel, tuple(order), sizes), out_shape=...  23.4 us
    pallas_call x1, Pallas kernels, body(): pl.pallas_call(write_outputs, out_shape=(jax.ShapeDtypeStruct((1, share,...  9.09 us

profile of v2, /device:TPU:1, one launch (start us, length us, event | category | flops | bytes accessed | tf_op | source)
XLA Modules:
  0.0 33.2 jit_solution(8073282920263793016)
XLA Ops:
  0.6 23.4 %shard_map.229 = (f32[64,512]{1,0:T(8,128)}, f32[64,512]{1,0:T(8,128)}, f32[4]{0:T(128)}) custom-call(bf16[512,512]{1,0:T(8,128)(2,1)} %refs_0_.1, bf16[512,128]{1,0:T(8,128)(2,1)} %constant.30.clone.refs_1_, s32[2,4]{1,0:T(2,128)} %bitcast.5, s32[4]{0:T(128)} %refs_3_.1, f32[4]{0:T(128)} %refs_4_.1, f32[2,2,4]{2,1,0:T(2,128)} %bitcast.4, ...), custom_call_target="tpu_custom_call" | custom-call | tf_op jit(solution)/shard_map/pallas_call | solution.py:448
  24.1 9.1 %shard_map.230 = (f32[1,64,512]{2,1,0:T(8,128)}, f32[1,64,512]{2,1,0:T(8,128)}, f32[4]{0:T(128)}) custom-call(f32[64,512]{1,0:T(8,128)} %get-tuple-element.6.image, f32[64,512]{1,0:T(8,128)} %get-tuple-element.7.grad, f32[4]{0:T(128)} %get-tuple-element.8.source), custom_call_target="tpu_custom_call" | custom-call | tf_op jit(solution)/shard_map/pallas_call | solution.py:462

commit v3 on v2

--- a/solution.py
+++ b/solution.py
@@ -81,6 +81,8 @@
 
 
 SCALARS = ("offsets", "ids", "weights", "polar")
+FIRST = ("mask", "col_fwd")
+SECOND = SCALARS + ("jones", "row_fwd", "row_amb", "col_inv", "row_inv")
 OWN_ROWS = ("d_row", "row_back", "amb_back")
 
 
@@ -107,6 +109,24 @@
     tile = lax.axis_index("tile")
     other = 1 - tile
 
+    own = pl.ds(pl.multiple_of(me * share, share), share)
+    loads = {}
+
+    def load(chosen):
+        for i, name in enumerate(names):
+            if name not in chosen:
+                continue
+            source = hbm[name]
+            if name == "amb_back":
+                source = source.at[tile, own]
+            elif name == "row_amb":
+                source = source.at[tile]
+            elif name in OWN_ROWS:
+                source = source.at[own]
+            loads[name] = pltpu.make_async_copy(source, vmem[name], load_sem.at[i])
+            loads[name].start()
+
+    load(FIRST)
     barrier = pltpu.get_barrier_semaphore()
     for step in range(n):
         peer = lax.rem(me + step, n)
@@ -114,24 +134,22 @@
             pl.semaphore_signal(barrier, inc=1, device_id={"src": peer, "tile": tile})
         pl.semaphore_signal(barrier, inc=1, device_id={"src": peer, "tile": other})
 
-    own = pl.ds(pl.multiple_of(me * share, share), share)
-    loads = {}
-    for i, name in enumerate(names):
-        source = hbm[name]
-        if name == "amb_back":
-            source = source.at[tile, own]
-        elif name == "row_amb":
-            source = source.at[tile]
-        elif name in OWN_ROWS:
-            source = source.at[own]
-        loads[name] = pltpu.make_async_copy(source, vmem[name], load_sem.at[i])
-        loads[name].start()
+    load(SECOND)
 
     def table(name):
         loads[name].wait()
         return vmem[name][...]
 
     partial[...] = dot(table("mask"), table("col_fwd")).astype(jnp.bfloat16)
+    pl.semaphore_wait(barrier, 2 * n - 1)
+    rim = pl.ds(pl.multiple_of(other * (th - AMB), ROWS_16), AMB)
+    halo_copy = pltpu.make_async_remote_copy(
+        src_ref=partial.at[rim], dst_ref=halo, send_sem=halo_sem.at[0], recv_sem=halo_sem.at[1],
+        device_id={"tile": other},
+    )
+    halo_copy.start()
+    load([name for name in names if name not in FIRST + SECOND])
+
     for name in SCALARS + ("jones",):
         loads[name].wait()
     jones = vmem["jones"]
@@ -155,17 +173,7 @@
                     left, pltpu.roll(value, low, 1), pltpu.roll(value, high, 1)
                 )
 
-    pl.semaphore_wait(barrier, 2 * n - 1)
-    rim = pl.ds(pl.multiple_of(other * (th - AMB), ROWS_16), AMB)
-    halo_copy = pltpu.make_async_remote_copy(
-        src_ref=partial.at[rim], dst_ref=halo, send_sem=halo_sem.at[0], recv_sem=halo_sem.at[1],
-        device_id={"tile": other},
-    )
-    halo_copy.start()
     product = dot(table("row_fwd"), partial[...])
-
-    projected = dot(table("target").astype(jnp.bfloat16), table("d_col_t")).astype(jnp.bfloat16)
-    target_small[...] = dot(table("d_row_t"), projected)
 
     halo_copy.wait()
     product = product + dot(table("row_amb"), halo[...])
@@ -174,26 +182,24 @@
     spec = norm * (product[:K] + sign * pltpu.roll(product[K:], K, 1))
     turned = -sign * pltpu.roll(spec, K, 1)
 
-    col_inv = table("col_inv")
-    row_inv = table("row_inv")
+    fields = 3 * local
+    masked = [
+        pupil_a[q * K : (q + 1) * K] * spec + pupil_b[q * K : (q + 1) * K] * turned
+        for q in range(fields)
+    ]
+    cols = dot(jnp.concatenate(masked, 0).astype(jnp.bfloat16), table("col_inv"))
+    cols = cols.astype(jnp.bfloat16)
+    mixed = [
+        jnp.concatenate([cols[q * K : (q + 1) * K, :grid], cols[q * K : (q + 1) * K, grid:]], 0)
+        for q in range(fields)
+    ]
+    field[...] = dot(table("row_inv"), jnp.concatenate(mixed, 1))
     total = jnp.zeros((grid, grid), jnp.float32)
     for s in range(local):
-        masked = [
-            pupil_a[q * K : (q + 1) * K] * spec + pupil_b[q * K : (q + 1) * K] * turned
-            for q in range(3 * s, 3 * s + 3)
-        ]
-        cols = dot(jnp.concatenate(masked, 0).astype(jnp.bfloat16), col_inv).astype(jnp.bfloat16)
-        mixed = jnp.concatenate(
-            [
-                jnp.concatenate([cols[j * K : (j + 1) * K, :grid], cols[j * K : (j + 1) * K, grid:]], 0)
-                for j in range(3)
-            ],
-            1,
-        )
-        values = dot(row_inv, mixed)
-        field[s] = values
-        squares = values[:grid] * values[:grid] + values[grid:] * values[grid:]
-        power_s = squares[:, :grid] + squares[:, grid : 2 * grid] + squares[:, 2 * grid :]
+        power_s = jnp.zeros((grid, grid), jnp.float32)
+        for q in range(3 * s, 3 * s + 3):
+            values = field[:, q * grid : (q + 1) * grid]
+            power_s = power_s + values[:grid] * values[:grid] + values[grid:] * values[grid:]
         power[s] = power_s
         total = total + (weights[s] / parts_total) * power_s
     part[...] = total.astype(jnp.bfloat16)
@@ -236,6 +242,9 @@
             send_sem=gather_send.at[step], recv_sem=gather_recv.at[step],
             device_id={"src": peer},
         )
+    projected = dot(table("target").astype(jnp.bfloat16), table("d_col_t")).astype(jnp.bfloat16)
+    target_small[...] = dot(table("d_row_t"), projected)
+
     guarded(me < owners, reduce_own)
     row_inv_t = table("row_inv_t")
     col_back = table("col_back")
@@ -249,29 +258,22 @@
     residual = dot(gram, twice) - target_small[...]
     doubled = jnp.concatenate([residual, residual], 0)
 
+    scaled = [
+        (doubled * field[:, q * grid : (q + 1) * grid]).astype(jnp.bfloat16) for q in range(fields)
+    ]
+    rows = dot(row_inv_t, jnp.concatenate(scaled, 1)).astype(jnp.bfloat16)
+    mixed = [
+        jnp.concatenate([rows[:K, q * grid : (q + 1) * grid], rows[K:, q * grid : (q + 1) * grid]], 1)
+        for q in range(fields)
+    ]
+    both = dot(jnp.concatenate(mixed, 0), col_back)
     grad = jnp.zeros((K, LANES), jnp.float32)
     scale = 2.0 / (parts_total * K)
     for s in range(local):
-        values = field[s]
-        scaled = jnp.concatenate(
-            [doubled * values[:, j * grid : (j + 1) * grid] for j in range(3)], 1
-        ).astype(jnp.bfloat16)
-        rows = dot(row_inv_t, scaled).astype(jnp.bfloat16)
-        mixed = jnp.concatenate(
-            [
-                jnp.concatenate(
-                    [rows[:K, j * grid : (j + 1) * grid], rows[K:, j * grid : (j + 1) * grid]], 1
-                )
-                for j in range(3)
-            ],
-            0,
-        )
-        both = dot(mixed, col_back)
         own_grad = jnp.zeros((K, LANES), jnp.float32)
-        for j in range(3):
-            q = 3 * s + j
+        for q in range(3 * s, 3 * s + 3):
             rows_q = slice(q * K, (q + 1) * K)
-            pair = both[j * K : (j + 1) * K]
+            pair = both[rows_q]
             own_grad = own_grad + pupil_a[rows_q] * pair[:, :LANES] + pupil_b[rows_q] * pair[:, LANES:]
         grad = grad + (scale * weights[s]) * own_grad
     spec_send[...] = (norm * grad).astype(jnp.bfloat16)
@@ -358,16 +360,21 @@
         copy.wait()
 
 
-def write_outputs(image, grad, source, image_out, grad_out, source_out, sem):
-    copies = [
-        pltpu.make_async_copy(image, image_out.at[0], sem.at[0]),
-        pltpu.make_async_copy(grad, grad_out.at[0], sem.at[1]),
-        pltpu.make_async_copy(source, source_out, sem.at[2]),
-    ]
-    for copy in copies:
-        copy.start()
-    for copy in copies:
-        copy.wait()
+def write_outputs(image, grad, source, image_out, grad_out, source_out, held, scalars, sem):
+    ways = [
+        (image, held.at[0], image_out.at[0]),
+        (grad, held.at[1], grad_out.at[0]),
+        (source, scalars, source_out),
+    ]
+    loads = [pltpu.make_async_copy(w[0], w[1], sem.at[0, i]) for i, w in enumerate(ways)]
+    stores = [pltpu.make_async_copy(w[1], w[2], sem.at[1, i]) for i, w in enumerate(ways)]
+    for load in loads:
+        load.start()
+    for load, store in zip(loads, stores):
+        load.wait()
+        store.start()
+    for store in stores:
+        store.wait()
 
 
 def body(
@@ -415,7 +422,7 @@
         pltpu.VMEM((AMB, LANES), bf16),
         pltpu.VMEM((3 * local * K, LANES), f32),
         pltpu.VMEM((3 * local * K, LANES), f32),
-        pltpu.VMEM((local, 2 * grid, 3 * grid), f32),
+        pltpu.VMEM((2 * grid, 3 * local * grid), f32),
         pltpu.VMEM((local, grid, grid), f32),
         pltpu.VMEM((grid, grid), f32),
         pltpu.VMEM((grid, grid), bf16),
@@ -468,7 +475,7 @@
         ),
         in_specs=[in_hbm] * 3,
         out_specs=(in_hbm,) * 3,
-        scratch_shapes=[sems((3,))],
+        scratch_shapes=[pltpu.VMEM((2, share, tw), f32), pltpu.SMEM((local,), f32), sems((2, 3))],
         compiler_params=pltpu.CompilerParams(vmem_limit_bytes=VMEM_LIMIT),
     )(*results)
 

time: 33.3 us -> 24.7 us (0.74)
  Pallas kernels: 32.5 us -> 23.9 us
    pallas_call x1, Pallas kernels: 9.09 us -> 1.68 us  [body(): pl.pallas_call(write_outputs, out_shape=(jax.ShapeDtypeStruct((1, share,...]
    pallas_call x1, Pallas kernels: 23.4 us -> 22.2 us  [body(): pl.pallas_call(functools.partial(kernel, tuple(order), sizes), out_shape=...]
where the time goes in v3:
time: 24.7 us; the launch traced here: 24.5 us
  Pallas kernels  23.9 us (97%)
  between operations  0.64 us (3%)
    pallas_call x1, Pallas kernels, body(): pl.pallas_call(functools.partial(kernel, tuple(order), sizes), out_shape=...  22.2 us
    pallas_call x1, Pallas kernels, body(): pl.pallas_call(write_outputs, out_shape=(jax.ShapeDtypeStruct((1, share,...  1.68 us

profile of v3, /device:TPU:1, one launch (start us, length us, event | category | flops | bytes accessed | tf_op | source)
XLA Modules:
  0.0 24.5 jit_solution(7873686296361149554)
XLA Ops:
  0.6 22.2 %shard_map.229 = (f32[64,512]{1,0:T(8,128)}, f32[64,512]{1,0:T(8,128)}, f32[4]{0:T(128)}) custom-call(bf16[512,512]{1,0:T(8,128)(2,1)} %refs_0_.1, bf16[512,128]{1,0:T(8,128)(2,1)} %constant.30.clone.refs_1_, s32[2,4]{1,0:T(2,128)} %bitcast.5, s32[4]{0:T(128)} %refs_3_.1, f32[4]{0:T(128)} %refs_4_.1, f32[2,2,4]{2,1,0:T(2,128)} %bitcast.4, ...), custom_call_target="tpu_custom_call" | custom-call | tf_op jit(solution)/shard_map/pallas_call | solution.py:455
  22.9 1.7 %shard_map.230 = (f32[1,64,512]{2,1,0:T(8,128)}, f32[1,64,512]{2,1,0:T(8,128)}, f32[4]{0:T(128)}) custom-call(f32[64,512]{1,0:T(8,128)} %get-tuple-element.6.image, f32[64,512]{1,0:T(8,128)} %get-tuple-element.7.grad, f32[4]{0:T(128)} %get-tuple-element.8.source), custom_call_target="tpu_custom_call" | custom-call | tf_op jit(solution)/shard_map/pallas_call | solution.py:469

commit v4 on v3

--- a/solution.py
+++ b/solution.py
@@ -61,29 +61,26 @@
     d_row = dirichlet((np.arange(th) + AMB) / window)
     d_col = dirichlet(np.arange(tw) / tw)
     gram = (tw / grid) * (d_row.T @ d_row)
+    cat = lambda *parts: np.concatenate(parts, 1)
+    wide_early = cat(bf(row_fwd[:, AMB : AMB + th]), bf(col_inv / K))
+    wide_late = cat(bf(d_row.T), *split_bf16(gram), bf(row_inv.T), bf(col_fwd.T))
+    tall_late = cat(bf(col_back), bf(np.concatenate([d_col.T, d_col.T], 0)))
+    own_rows = cat(*split_bf16(d_row), bf(row_back))
     return dict(
         col_fwd=bf(col_fwd),
-        row_fwd=bf(row_fwd[:, AMB : AMB + th]),
+        wide_early=wide_early,
         row_amb=bf(row_amb),
+        row_inv=bf(row_inv),
         d_col_t=bf(d_col),
-        d_row_t=bf(d_row.T),
-        col_inv=bf(col_inv / K),
-        row_inv=bf(row_inv),
-        gram=np.concatenate(split_bf16(gram), 1),
-        row_inv_t=bf(row_inv.T),
-        col_back=bf(col_back),
-        d_col=bf(np.concatenate([d_col.T, d_col.T], 0)),
-        col_fwd_t=bf(col_fwd.T),
-        d_row=np.concatenate(split_bf16(d_row), 1),
-        row_back=bf(row_back),
+        wide_late=wide_late,
+        tall_late=tall_late,
+        own_rows=own_rows,
         amb_back=bf(amb_back),
     )
 
 
 SCALARS = ("offsets", "ids", "weights", "polar")
-FIRST = ("mask", "col_fwd")
-SECOND = SCALARS + ("jones", "row_fwd", "row_amb", "col_inv", "row_inv")
-OWN_ROWS = ("d_row", "row_back", "amb_back")
+FIRST = ("rim", "col_fwd", "mask")
 
 
 def dot(a, b):
@@ -99,7 +96,7 @@
     vmem = dict(zip(names, refs[3 + count : 3 + 2 * count]))
     offsets, ids, weights, polar = (vmem[name] for name in SCALARS)
     (
-        partial, halo, pupil_a, pupil_b, field, power, target_small,
+        rim_rows, rim_send, halo, pupil_a, pupil_b, field, power, target_small,
         part, landed, reduced, whole, spec_send, spec_land, edge_land, sums, sums_land,
         load_sem, halo_sem, scatter_send, scatter_recv, gather_send, gather_recv,
         spec_ssem, spec_rsem, edge_ssem, edge_rsem, sums_sem,
@@ -110,20 +107,21 @@
     other = 1 - tile
 
     own = pl.ds(pl.multiple_of(me * share, share), share)
+    rim = pl.ds(pl.multiple_of(other * (th - AMB), ROWS_16), AMB)
+    parts_of = {
+        "rim": lambda ref: ref.at[rim],
+        "amb_back": lambda ref: ref.at[tile, own],
+        "row_amb": lambda ref: ref.at[tile],
+        "own_rows": lambda ref: ref.at[own],
+    }
     loads = {}
 
     def load(chosen):
-        for i, name in enumerate(names):
-            if name not in chosen:
-                continue
-            source = hbm[name]
-            if name == "amb_back":
-                source = source.at[tile, own]
-            elif name == "row_amb":
-                source = source.at[tile]
-            elif name in OWN_ROWS:
-                source = source.at[own]
-            loads[name] = pltpu.make_async_copy(source, vmem[name], load_sem.at[i])
+        for name in chosen:
+            source = hbm["mask" if name == "rim" else name]
+            source = parts_of[name](source) if name in parts_of else source
+            target = rim_rows if name == "rim" else vmem[name]
+            loads[name] = pltpu.make_async_copy(source, target, load_sem.at[len(loads)])
             loads[name].start()
 
     load(FIRST)
@@ -133,22 +131,24 @@
         if step:
             pl.semaphore_signal(barrier, inc=1, device_id={"src": peer, "tile": tile})
         pl.semaphore_signal(barrier, inc=1, device_id={"src": peer, "tile": other})
-
-    load(SECOND)
-
-    def table(name):
-        loads[name].wait()
-        return vmem[name][...]
-
-    partial[...] = dot(table("mask"), table("col_fwd")).astype(jnp.bfloat16)
+    load([name for name in names if name not in FIRST])
+    waited = set()
+
+    def table(name, start=0, stop=None):
+        if name not in waited:
+            loads[name].wait()
+            waited.add(name)
+        return vmem[name][:, start:stop]
+
+    loads["rim"].wait()
+    rim_send[...] = dot(rim_rows[...], table("col_fwd")).astype(jnp.bfloat16)
     pl.semaphore_wait(barrier, 2 * n - 1)
-    rim = pl.ds(pl.multiple_of(other * (th - AMB), ROWS_16), AMB)
     halo_copy = pltpu.make_async_remote_copy(
-        src_ref=partial.at[rim], dst_ref=halo, send_sem=halo_sem.at[0], recv_sem=halo_sem.at[1],
+        src_ref=rim_send, dst_ref=halo, send_sem=halo_sem.at[0], recv_sem=halo_sem.at[1],
         device_id={"tile": other},
     )
     halo_copy.start()
-    load([name for name in names if name not in FIRST + SECOND])
+    partial = dot(table("mask"), table("col_fwd")).astype(jnp.bfloat16)
 
     for name in SCALARS + ("jones",):
         loads[name].wait()
@@ -173,7 +173,7 @@
                     left, pltpu.roll(value, low, 1), pltpu.roll(value, high, 1)
                 )
 
-    product = dot(table("row_fwd"), partial[...])
+    product = dot(table("wide_early", 0, th), partial)
 
     halo_copy.wait()
     product = product + dot(table("row_amb"), halo[...])
@@ -187,7 +187,7 @@
         pupil_a[q * K : (q + 1) * K] * spec + pupil_b[q * K : (q + 1) * K] * turned
         for q in range(fields)
     ]
-    cols = dot(jnp.concatenate(masked, 0).astype(jnp.bfloat16), table("col_inv"))
+    cols = dot(jnp.concatenate(masked, 0).astype(jnp.bfloat16), table("wide_early", th))
     cols = cols.astype(jnp.bfloat16)
     mixed = [
         jnp.concatenate([cols[q * K : (q + 1) * K, :grid], cols[q * K : (q + 1) * K, grid:]], 0)
@@ -243,12 +243,12 @@
             device_id={"src": peer},
         )
     projected = dot(table("target").astype(jnp.bfloat16), table("d_col_t")).astype(jnp.bfloat16)
-    target_small[...] = dot(table("d_row_t"), projected)
+    target_small[...] = dot(table("wide_late", 0, th), projected)
 
     guarded(me < owners, reduce_own)
-    row_inv_t = table("row_inv_t")
-    col_back = table("col_back")
-    gram = table("gram")
+    row_inv_t = table("wide_late", th + 2 * grid, th + 4 * grid)
+    col_back = table("tall_late", 0, 4 * K)
+    gram = table("wide_late", th, th + 2 * grid)
     for step in range(1, n):
         origin = lax.rem(me + n - step, n)
         guarded(origin < owners, gather[step].wait_recv)
@@ -304,10 +304,10 @@
     )
     sums_copy.start()
 
-    lines = dot(table("d_row"), twice)
+    lines = dot(table("own_rows", 0, 2 * grid), twice)
     lines_high = lines.astype(jnp.bfloat16)
     lines_low = (lines - lines_high.astype(jnp.float32)).astype(jnp.bfloat16)
-    image_out[...] = dot(jnp.concatenate([lines_high, lines_low], 1), table("d_col"))
+    image_out[...] = dot(jnp.concatenate([lines_high, lines_low], 1), table("tall_late", 4 * K))
 
     writes = [
         pltpu.make_async_copy(source, to, out_sem.at[i])
@@ -315,7 +315,8 @@
     ]
     writes[0].start()
 
-    row_back, amb_back, col_fwd_t = table("row_back"), table("amb_back"), table("col_fwd_t")
+    row_back, amb_back = table("own_rows", 2 * grid), table("amb_back")
+    col_fwd_t = table("wide_late", th + 4 * grid)
     sums_copy.wait()
     both_sums = jnp.sum(sums[...] + sums_land[...], 1, keepdims=True) / (2 * th * tw)
     for s in range(local):
@@ -400,7 +401,7 @@
         polar=polar_states.transpose(1, 2, 0),
     )
     constants = tables(th, tw)
-    order = ["mask", "col_fwd", *SCALARS, "jones", "row_fwd", "target", "d_col_t", "d_row_t"]
+    order = ["mask", "col_fwd", *SCALARS, "jones", "wide_early", "row_amb", "row_inv", "target"]
     order += [name for name in constants if name not in order]
     arrays = []
     held = []
@@ -412,13 +413,14 @@
             shape = (share,) + shape[2:]
         elif name == "row_amb":
             shape = shape[1:]
-        elif name in OWN_ROWS:
+        elif name == "own_rows":
             shape = (share,) + shape[1:]
         held.append((pltpu.SMEM if name in SCALARS else pltpu.VMEM)(shape, value.dtype))
     f32, bf16 = jnp.float32, jnp.bfloat16
     sems = pltpu.SemaphoreType.DMA
     scratch = held + [
-        pltpu.VMEM((th, LANES), bf16),
+        pltpu.VMEM((AMB, tw), bf16),
+        pltpu.VMEM((AMB, LANES), bf16),
         pltpu.VMEM((AMB, LANES), bf16),
         pltpu.VMEM((3 * local * K, LANES), f32),
         pltpu.VMEM((3 * local * K, LANES), f32),
@@ -434,7 +436,7 @@
         pltpu.VMEM((n, K, LANES), bf16),
         pltpu.VMEM((local, LANES), f32),
         pltpu.VMEM((local, LANES), f32),
-        sems((len(order),)),
+        sems((len(order) + 1,)),
         sems((2,)),
         sems((n,)),
         sems((n,)),

time: 24.7 us -> 24.5 us (level)
  no operation moved by 1% of the time
where the time goes in v4:
time: 24.5 us; the launch traced here: 24.3 us
  Pallas kernels  23.7 us (97%)
  between operations  0.64 us (3%)
    pallas_call x1, Pallas kernels, body(): pl.pallas_call(functools.partial(kernel, tuple(order), sizes), out_shape=...  22 us
    pallas_call x1, Pallas kernels, body(): pl.pallas_call(write_outputs, out_shape=(jax.ShapeDtypeStruct((1, share,...  1.68 us

profile of v4, /device:TPU:1, one launch (start us, length us, event | category | flops | bytes accessed | tf_op | source)
XLA Modules:
  0.0 24.3 jit_solution(9256259131040093529)
XLA Ops:
  0.6 22.0 %shard_map.175 = (f32[64,512]{1,0:T(8,128)}, f32[64,512]{1,0:T(8,128)}, f32[4]{0:T(128)}) custom-call(bf16[512,512]{1,0:T(8,128)(2,1)} %refs_0_.1, bf16[512,128]{1,0:T(8,128)(2,1)} %constant.18.clone.refs_1_, s32[2,4]{1,0:T(2,128)} %bitcast.5, s32[4]{0:T(128)} %refs_3_.1, f32[4]{0:T(128)} %refs_4_.1, f32[2,2,4]{2,1,0:T(2,128)} %bitcast.4, ...), custom_call_target="tpu_custom_call" | custom-call | tf_op jit(solution)/shard_map/pallas_call | solution.py:457
  22.7 1.7 %shard_map.176 = (f32[1,64,512]{2,1,0:T(8,128)}, f32[1,64,512]{2,1,0:T(8,128)}, f32[4]{0:T(128)}) custom-call(f32[64,512]{1,0:T(8,128)} %get-tuple-element.6.image, f32[64,512]{1,0:T(8,128)} %get-tuple-element.7.grad, f32[4]{0:T(128)} %get-tuple-element.8.source), custom_call_target="tpu_custom_call" | custom-call | tf_op jit(solution)/shard_map/pallas_call | solution.py:471

commit v5 on v4

--- a/solution.py
+++ b/solution.py
@@ -97,7 +97,7 @@
     offsets, ids, weights, polar = (vmem[name] for name in SCALARS)
     (
         rim_rows, rim_send, halo, pupil_a, pupil_b, field, power, target_small,
-        part, landed, reduced, whole, spec_send, spec_land, edge_land, sums, sums_land,
+        part, landed, reduced, whole, spec_send, spec_land, spec_half, half_land, sums, sums_land,
         load_sem, halo_sem, scatter_send, scatter_recv, gather_send, gather_recv,
         spec_ssem, spec_rsem, edge_ssem, edge_rsem, sums_sem,
         image_out, grad_out, source_out, out_sem,
@@ -126,10 +126,12 @@
 
     load(FIRST)
     barrier = pltpu.get_barrier_semaphore()
-    for step in range(n):
+    half = n // 2
+    twin = lax.rem(me + half, n)
+    for step in range(1, n):
         peer = lax.rem(me + step, n)
-        if step:
-            pl.semaphore_signal(barrier, inc=1, device_id={"src": peer, "tile": tile})
+        pl.semaphore_signal(barrier, inc=1, device_id={"src": peer, "tile": tile})
+    for peer in (me, twin):
         pl.semaphore_signal(barrier, inc=1, device_id={"src": peer, "tile": other})
     load([name for name in names if name not in FIRST])
     waited = set()
@@ -142,7 +144,7 @@
 
     loads["rim"].wait()
     rim_send[...] = dot(rim_rows[...], table("col_fwd")).astype(jnp.bfloat16)
-    pl.semaphore_wait(barrier, 2 * n - 1)
+    pl.semaphore_wait(barrier, n + 1)
     halo_copy = pltpu.make_async_remote_copy(
         src_ref=rim_send, dst_ref=halo, send_sem=halo_sem.at[0], recv_sem=halo_sem.at[1],
         device_id={"tile": other},
@@ -278,24 +280,15 @@
         grad = grad + (scale * weights[s]) * own_grad
     spec_send[...] = (norm * grad).astype(jnp.bfloat16)
 
-    spread, rims = {}, []
-    for step in range(1, n):
-        peer = lax.rem(me + step, n)
+    spread = {}
+    start_half = me - lax.rem(me, half)
+    for step in range(1, half):
         spread[step] = pltpu.make_async_remote_copy(
             src_ref=spec_send, dst_ref=spec_land.at[step],
             send_sem=spec_ssem.at[step], recv_sem=spec_rsem.at[step],
-            device_id={"src": peer},
+            device_id={"src": start_half + lax.rem(me + step, half)},
         )
         spread[step].start()
-    for e in range(edges):
-        rims.append(
-            pltpu.make_async_remote_copy(
-                src_ref=spec_send, dst_ref=edge_land.at[me],
-                send_sem=edge_ssem.at[e], recv_sem=edge_rsem.at[me],
-                device_id={"src": e + tile * (n - edges), "tile": other},
-            )
-        )
-        rims[-1].start()
     for s in range(local):
         sums[s : s + 1, :] = jnp.sum(residual * power[s], 0, keepdims=True)
     sums_copy = pltpu.make_async_remote_copy(
@@ -307,6 +300,33 @@
     lines = dot(table("own_rows", 0, 2 * grid), twice)
     lines_high = lines.astype(jnp.bfloat16)
     lines_low = (lines - lines_high.astype(jnp.float32)).astype(jnp.bfloat16)
+    def stack(value):
+        return jnp.concatenate([value, -sign * pltpu.roll(value, K, 1)], 0).astype(jnp.bfloat16)
+
+    summed = spec_send[...].astype(jnp.float32)
+    for step in range(1, half):
+        spread[step].wait_recv()
+        summed = summed + spec_land[step].astype(jnp.float32)
+
+    spec_half[...] = summed.astype(jnp.bfloat16)
+
+    def half_copy(slot, where):
+        return pltpu.make_async_remote_copy(
+            src_ref=spec_half, dst_ref=half_land.at[slot],
+            send_sem=edge_ssem.at[slot], recv_sem=edge_rsem.at[slot], device_id=where,
+        )
+
+    def at_rim(index, which):
+        return jnp.where(which == 0, index >= n - edges, index < edges)
+
+    to_twin = half_copy(0, {"src": twin, "tile": tile})
+    to_twin.start()
+    rims = [
+        (at_rim(twin, other), half_copy(1, {"src": twin, "tile": other})),
+        (at_rim(me, other), half_copy(2, {"src": me, "tile": other})),
+    ]
+    for condition, copy in rims:
+        pl.when(condition)(copy.start)
     image_out[...] = dot(jnp.concatenate([lines_high, lines_low], 1), table("tall_late", 4 * K))
 
     writes = [
@@ -323,40 +343,31 @@
         source_out[s] = both_sums[s, 0]
     writes[2].start()
 
-    def stack(value):
-        return jnp.concatenate([value, -sign * pltpu.roll(value, K, 1)], 0).astype(jnp.bfloat16)
-
-    summed = spec_send[...].astype(jnp.float32)
-    for step in range(1, n):
-        spread[step].wait_recv()
-        summed = summed + spec_land[step].astype(jnp.float32)
+    to_twin.wait_recv()
+    summed = summed + half_land[0].astype(jnp.float32)
     rows = dot(row_back, stack(summed))
-    at_rim = jnp.where(tile == 0, me >= n - edges, me < edges)
-
-    @pl.when(at_rim)
+
+    @pl.when(at_rim(me, tile))
     def _():
-        outer = jnp.zeros((K, LANES), jnp.float32)
-        for d in range(n):
-            pltpu.make_async_remote_copy(
-                src_ref=spec_send, dst_ref=edge_land.at[d],
-                send_sem=edge_ssem.at[0], recv_sem=edge_rsem.at[d],
-                device_id={"tile": other},
-            ).wait_recv()
-            outer = outer + edge_land[d].astype(jnp.float32)
+        for _, copy in rims:
+            copy.wait_recv()
+        outer = half_land[1].astype(jnp.float32) + half_land[2].astype(jnp.float32)
         full = rows + dot(amb_back, stack(outer))
         grad_out[...] = GRAD_SCALE * dot(full.astype(jnp.bfloat16), col_fwd_t)
 
-    @pl.when(jnp.logical_not(at_rim))
+    @pl.when(jnp.logical_not(at_rim(me, tile)))
     def _():
         grad_out[...] = GRAD_SCALE * dot(rows.astype(jnp.bfloat16), col_fwd_t)
 
     writes[1].start()
+    to_twin.wait_send()
+    for condition, copy in rims:
+        pl.when(condition)(copy.wait_send)
+    for step in range(1, half):
+        spread[step].wait_send()
     for step in range(1, n):
         guarded(lax.rem(me + step, n) < owners, scatter[step].wait_send)
         guarded(me < owners, gather[step].wait_send)
-        spread[step].wait_send()
-    for copy in rims:
-        copy.wait_send()
     for copy in writes:
         copy.wait()
 
@@ -383,7 +394,7 @@
 ):
     th, tw = mask_values.shape
     n = lax.axis_size("src")
-    assert lax.axis_size("tile") == 2
+    assert lax.axis_size("tile") == 2 and n % 2 == 0
     local = source_weights.shape[0]
     share = th // n
     grid = 2 * K
@@ -432,8 +443,9 @@
         pltpu.VMEM((block_rows, grid), bf16),
         pltpu.VMEM((grid, grid), bf16),
         pltpu.VMEM((K, LANES), bf16),
-        pltpu.VMEM((n, K, LANES), bf16),
-        pltpu.VMEM((n, K, LANES), bf16),
+        pltpu.VMEM((n // 2, K, LANES), bf16),
+        pltpu.VMEM((K, LANES), bf16),
+        pltpu.VMEM((3, K, LANES), bf16),
         pltpu.VMEM((local, LANES), f32),
         pltpu.VMEM((local, LANES), f32),
         sems((len(order) + 1,)),
@@ -442,10 +454,10 @@
         sems((n,)),
         sems((n,)),
         sems((n,)),
-        sems((n,)),
-        sems((n,)),
-        sems((edges,)),
-        sems((n,)),
+        sems((n // 2,)),
+        sems((n // 2,)),
+        sems((3,)),
+        sems((3,)),
         sems((2,)),
         pltpu.VMEM((share, tw), f32),
         pltpu.VMEM((share, tw), f32),

time: 24.5 us -> 26.1 us (1.065); the launches traced: 24.3 us -> 25.6 us
  Pallas kernels: 23.7 us -> 24.9 us
    pallas_call x1, Pallas kernels: 22 us -> 23.3 us  [body(): pl.pallas_call(functools.partial(kernel, tuple(order), sizes), out_shape=...]
where the time goes in v5:
time: 26.1 us; the launch traced here: 25.6 us
  Pallas kernels  24.9 us (95%)
  between operations  0.64 us (2%)
    pallas_call x1, Pallas kernels, body(): pl.pallas_call(functools.partial(kernel, tuple(order), sizes), out_shape=...  23.3 us
    pallas_call x1, Pallas kernels, body(): pl.pallas_call(write_outputs, out_shape=(jax.ShapeDtypeStruct((1, share,...  1.68 us

profile of v5, /device:TPU:1, one launch (start us, length us, event | category | flops | bytes accessed | tf_op | source)
XLA Modules:
  0.0 25.6 jit_solution(2907796112589420878)
XLA Ops:
  0.6 23.3 %shard_map.175 = (f32[64,512]{1,0:T(8,128)}, f32[64,512]{1,0:T(8,128)}, f32[4]{0:T(128)}) custom-call(bf16[512,512]{1,0:T(8,128)(2,1)} %refs_0_.1, bf16[512,128]{1,0:T(8,128)(2,1)} %constant.18.clone.refs_1_, s32[2,4]{1,0:T(2,128)} %bitcast.5, s32[4]{0:T(128)} %refs_3_.1, f32[4]{0:T(128)} %refs_4_.1, f32[2,2,4]{2,1,0:T(2,128)} %bitcast.4, ...), custom_call_target="tpu_custom_call" | custom-call | tf_op jit(solution)/shard_map/pallas_call | solution.py:469
  23.9 1.7 %shard_map.176 = (f32[1,64,512]{2,1,0:T(8,128)}, f32[1,64,512]{2,1,0:T(8,128)}, f32[4]{0:T(128)}) custom-call(f32[64,512]{1,0:T(8,128)} %get-tuple-element.6.image, f32[64,512]{1,0:T(8,128)} %get-tuple-element.7.grad, f32[4]{0:T(128)} %get-tuple-element.8.source), custom_call_target="tpu_custom_call" | custom-call | tf_op jit(solution)/shard_map/pallas_call | solution.py:483

commit v6 on v4

--- a/solution.py
+++ b/solution.py
@@ -88,7 +88,7 @@
 
 
 def kernel(names, sizes, *refs):
-    n, local, th, tw, share, owners, block_rows, edges, parts_total = sizes
+    n, local, th, tw, share, edges, parts_total = sizes
     grid = 2 * K
     count = len(names)
     hbm = dict(zip(names, refs[:count]))
@@ -97,8 +97,8 @@
     offsets, ids, weights, polar = (vmem[name] for name in SCALARS)
     (
         rim_rows, rim_send, halo, pupil_a, pupil_b, field, power, target_small,
-        part, landed, reduced, whole, spec_send, spec_land, edge_land, sums, sums_land,
-        load_sem, halo_sem, scatter_send, scatter_recv, gather_send, gather_recv,
+        part, landed, spec_send, spec_land, edge_land, sums, sums_land,
+        load_sem, halo_sem, gather_send, gather_recv,
         spec_ssem, spec_rsem, edge_ssem, edge_rsem, sums_sem,
         image_out, grad_out, source_out, out_sem,
     ) = refs[3 + 2 * count :]
@@ -204,56 +204,27 @@
         total = total + (weights[s] / parts_total) * power_s
     part[...] = total.astype(jnp.bfloat16)
 
-    def block(index):
-        return pl.ds(pl.multiple_of(index * block_rows, block_rows), block_rows)
-
-    def guarded(condition, run):
-        if owners == n:
-            run()
-        else:
-            pl.when(condition)(run)
-
-    scatter, gather = {}, {}
-    for step in range(1, n):
-        peer = lax.rem(me + step, n)
-        to = peer if owners == n else jnp.minimum(peer, owners - 1)
-        scatter[step] = pltpu.make_async_remote_copy(
-            src_ref=part.at[block(to)], dst_ref=landed.at[step],
-            send_sem=scatter_send.at[step], recv_sem=scatter_recv.at[step],
-            device_id={"src": peer},
+    order = sorted(range(1, n), key=lambda step: -min(step, n - step))
+    gather = {}
+    for step in order:
+        gather[step] = pltpu.make_async_remote_copy(
+            src_ref=part, dst_ref=landed.at[step],
+            send_sem=gather_send.at[step], recv_sem=gather_recv.at[step],
+            device_id={"src": lax.rem(me + step, n)},
         )
-        guarded(peer < owners, scatter[step].start)
-    mine = me if owners == n else jnp.minimum(me, owners - 1)
-
-    def reduce_own():
-        acc = part[block(mine), :].astype(jnp.float32)
-        for step in range(1, n):
-            scatter[step].wait_recv()
-            acc = acc + landed[step].astype(jnp.float32)
-        reduced[...] = acc.astype(jnp.bfloat16)
-        for step in range(1, n):
-            gather[step].start()
-        whole[block(mine), :] = reduced[...]
-
-    for step in range(1, n):
-        peer = lax.rem(me + step, n)
-        gather[step] = pltpu.make_async_remote_copy(
-            src_ref=reduced, dst_ref=whole.at[block(mine)],
-            send_sem=gather_send.at[step], recv_sem=gather_recv.at[step],
-            device_id={"src": peer},
-        )
+        gather[step].start()
+
     projected = dot(table("target").astype(jnp.bfloat16), table("d_col_t")).astype(jnp.bfloat16)
     target_small[...] = dot(table("wide_late", 0, th), projected)
 
-    guarded(me < owners, reduce_own)
     row_inv_t = table("wide_late", th + 2 * grid, th + 4 * grid)
     col_back = table("tall_late", 0, 4 * K)
     gram = table("wide_late", th, th + 2 * grid)
-    for step in range(1, n):
-        origin = lax.rem(me + n - step, n)
-        guarded(origin < owners, gather[step].wait_recv)
-
-    image = whole[...]
+    image = part[...].astype(jnp.float32)
+    for step in reversed(order):
+        gather[step].wait_recv()
+        image = image + landed[step].astype(jnp.float32)
+    image = image.astype(jnp.bfloat16)
     twice = jnp.concatenate([image, image], 0)
     residual = dot(gram, twice) - target_small[...]
     doubled = jnp.concatenate([residual, residual], 0)
@@ -279,14 +250,6 @@
     spec_send[...] = (norm * grad).astype(jnp.bfloat16)
 
     spread, rims = {}, []
-    for step in range(1, n):
-        peer = lax.rem(me + step, n)
-        spread[step] = pltpu.make_async_remote_copy(
-            src_ref=spec_send, dst_ref=spec_land.at[step],
-            send_sem=spec_ssem.at[step], recv_sem=spec_rsem.at[step],
-            device_id={"src": peer},
-        )
-        spread[step].start()
     for e in range(edges):
         rims.append(
             pltpu.make_async_remote_copy(
@@ -296,6 +259,14 @@
             )
         )
         rims[-1].start()
+    for step in order:
+        peer = lax.rem(me + step, n)
+        spread[step] = pltpu.make_async_remote_copy(
+            src_ref=spec_send, dst_ref=spec_land.at[step],
+            send_sem=spec_ssem.at[step], recv_sem=spec_rsem.at[step],
+            device_id={"src": peer},
+        )
+        spread[step].start()
     for s in range(local):
         sums[s : s + 1, :] = jnp.sum(residual * power[s], 0, keepdims=True)
     sums_copy = pltpu.make_async_remote_copy(
@@ -327,7 +298,7 @@
         return jnp.concatenate([value, -sign * pltpu.roll(value, K, 1)], 0).astype(jnp.bfloat16)
 
     summed = spec_send[...].astype(jnp.float32)
-    for step in range(1, n):
+    for step in reversed(order):
         spread[step].wait_recv()
         summed = summed + spec_land[step].astype(jnp.float32)
     rows = dot(row_back, stack(summed))
@@ -352,8 +323,7 @@
 
     writes[1].start()
     for step in range(1, n):
-        guarded(lax.rem(me + step, n) < owners, scatter[step].wait_send)
-        guarded(me < owners, gather[step].wait_send)
+        gather[step].wait_send()
         spread[step].wait_send()
     for copy in rims:
         copy.wait_send()
@@ -387,9 +357,6 @@
     local = source_weights.shape[0]
     share = th // n
     grid = 2 * K
-    owners = min(n, grid // ROWS_16)
-    block_rows = grid // owners
-    assert owners * block_rows == grid
     edges = -(-AMB // share)
     named = dict(
         mask=mask_values,
@@ -428,9 +395,7 @@
         pltpu.VMEM((local, grid, grid), f32),
         pltpu.VMEM((grid, grid), f32),
         pltpu.VMEM((grid, grid), bf16),
-        pltpu.VMEM((n, block_rows, grid), bf16),
-        pltpu.VMEM((block_rows, grid), bf16),
-        pltpu.VMEM((grid, grid), bf16),
+        pltpu.VMEM((n, grid, grid), bf16),
         pltpu.VMEM((K, LANES), bf16),
         pltpu.VMEM((n, K, LANES), bf16),
         pltpu.VMEM((n, K, LANES), bf16),
@@ -442,8 +407,6 @@
         sems((n,)),
         sems((n,)),
         sems((n,)),
-        sems((n,)),
-        sems((n,)),
         sems((edges,)),
         sems((n,)),
         sems((2,)),
@@ -452,7 +415,7 @@
         pltpu.SMEM((local,), f32),
         sems((3,)),
     ]
-    sizes = (n, local, th, tw, share, owners, block_rows, edges, local * n)
+    sizes = (n, local, th, tw, share, edges, local * n)
     in_hbm = pl.BlockSpec(memory_space=pltpu.HBM)
     results = pl.pallas_call(
         functools.partial(kernel, tuple(order), sizes),

time: 24.5 us -> 25.8 us (1.053)
  the two profiles are of different devices: /device:TPU:1 before, /device:TPU:0 now
where the time goes in v6:
time: 25.8 us; the launch traced here: 25.6 us
  Pallas kernels  25 us (97%)
  between operations  0.64 us (2%)
    pallas_call x1, Pallas kernels, body(): pl.pallas_call(functools.partial(kernel, tuple(order), sizes), out_shape=...  23.3 us
    pallas_call x1, Pallas kernels, body(): pl.pallas_call(write_outputs, out_shape=(jax.ShapeDtypeStruct((1, share,...  1.68 us

profile of v6, /device:TPU:0, one launch (start us, length us, event | category | flops | bytes accessed | tf_op | source)
XLA Modules:
  0.0 25.6 jit_solution(2506284572807109282)
XLA Ops:
  0.6 23.3 %shard_map.175 = (f32[64,512]{1,0:T(8,128)}, f32[64,512]{1,0:T(8,128)}, f32[4]{0:T(128)}) custom-call(bf16[512,512]{1,0:T(8,128)(2,1)} %refs_0_.1, bf16[512,128]{1,0:T(8,128)(2,1)} %constant.18.clone.refs_1_, s32[2,4]{1,0:T(2,128)} %bitcast.5, s32[4]{0:T(128)} %refs_3_.1, f32[4]{0:T(128)} %refs_4_.1, f32[2,2,4]{2,1,0:T(2,128)} %bitcast.4, ...), custom_call_target="tpu_custom_call" | custom-call | tf_op jit(solution)/shard_map/pallas_call | solution.py:420
  23.9 1.7 %shard_map.176 = (f32[1,64,512]{2,1,0:T(8,128)}, f32[1,64,512]{2,1,0:T(8,128)}, f32[4]{0:T(128)}) custom-call(f32[64,512]{1,0:T(8,128)} %get-tuple-element.6.image, f32[64,512]{1,0:T(8,128)} %get-tuple-element.7.grad, f32[4]{0:T(128)} %get-tuple-element.8.source), custom_call_target="tpu_custom_call" | custom-call | tf_op jit(solution)/shard_map/pallas_call | solution.py:434

commit v7 on v4

--- a/solution.py
+++ b/solution.py
@@ -124,13 +124,14 @@
             loads[name] = pltpu.make_async_copy(source, target, load_sem.at[len(loads)])
             loads[name].start()
 
+    order = sorted(range(1, n), key=lambda step: -min(step, n - step))
+    barrier = pltpu.get_barrier_semaphore()
+    pl.semaphore_signal(barrier, inc=1, device_id={"tile": other})
     load(FIRST)
-    barrier = pltpu.get_barrier_semaphore()
-    for step in range(n):
+    for step in order:
         peer = lax.rem(me + step, n)
-        if step:
-            pl.semaphore_signal(barrier, inc=1, device_id={"src": peer, "tile": tile})
-        pl.semaphore_signal(barrier, inc=1, device_id={"src": peer, "tile": other})
+        for which in (tile, other):
+            pl.semaphore_signal(barrier, inc=1, device_id={"src": peer, "tile": which})
     load([name for name in names if name not in FIRST])
     waited = set()
 
@@ -214,7 +215,7 @@
             pl.when(condition)(run)
 
     scatter, gather = {}, {}
-    for step in range(1, n):
+    for step in order:
         peer = lax.rem(me + step, n)
         to = peer if owners == n else jnp.minimum(peer, owners - 1)
         scatter[step] = pltpu.make_async_remote_copy(
@@ -227,11 +228,11 @@
 
     def reduce_own():
         acc = part[block(mine), :].astype(jnp.float32)
-        for step in range(1, n):
+        for step in reversed(order):
             scatter[step].wait_recv()
             acc = acc + landed[step].astype(jnp.float32)
         reduced[...] = acc.astype(jnp.bfloat16)
-        for step in range(1, n):
+        for step in order:
             gather[step].start()
         whole[block(mine), :] = reduced[...]
 
@@ -249,7 +250,7 @@
     row_inv_t = table("wide_late", th + 2 * grid, th + 4 * grid)
     col_back = table("tall_late", 0, 4 * K)
     gram = table("wide_late", th, th + 2 * grid)
-    for step in range(1, n):
+    for step in reversed(order):
         origin = lax.rem(me + n - step, n)
         guarded(origin < owners, gather[step].wait_recv)
 
@@ -279,14 +280,6 @@
     spec_send[...] = (norm * grad).astype(jnp.bfloat16)
 
     spread, rims = {}, []
-    for step in range(1, n):
-        peer = lax.rem(me + step, n)
-        spread[step] = pltpu.make_async_remote_copy(
-            src_ref=spec_send, dst_ref=spec_land.at[step],
-            send_sem=spec_ssem.at[step], recv_sem=spec_rsem.at[step],
-            device_id={"src": peer},
-        )
-        spread[step].start()
     for e in range(edges):
         rims.append(
             pltpu.make_async_remote_copy(
@@ -296,6 +289,14 @@
             )
         )
         rims[-1].start()
+    for step in order:
+        peer = lax.rem(me + step, n)
+        spread[step] = pltpu.make_async_remote_copy(
+            src_ref=spec_send, dst_ref=spec_land.at[step],
+            send_sem=spec_ssem.at[step], recv_sem=spec_rsem.at[step],
+            device_id={"src": peer},
+        )
+        spread[step].start()
     for s in range(local):
         sums[s : s + 1, :] = jnp.sum(residual * power[s], 0, keepdims=True)
     sums_copy = pltpu.make_async_remote_copy(
@@ -327,7 +328,7 @@
         return jnp.concatenate([value, -sign * pltpu.roll(value, K, 1)], 0).astype(jnp.bfloat16)
 
     summed = spec_send[...].astype(jnp.float32)
-    for step in range(1, n):
+    for step in reversed(order):
         spread[step].wait_recv()
         summed = summed + spec_land[step].astype(jnp.float32)
     rows = dot(row_back, stack(summed))

time: 24.5 us -> 25.2 us (1.029)
  the two profiles are of different devices: /device:TPU:1 before, /device:TPU:0 now
where the time goes in v7:
time: 25.2 us; the launch traced here: 25 us
  Pallas kernels  24.4 us (97%)
  between operations  0.64 us (3%)
    pallas_call x1, Pallas kernels, body(): pl.pallas_call(functools.partial(kernel, tuple(order), sizes), out_shape=...  22.7 us
    pallas_call x1, Pallas kernels, body(): pl.pallas_call(write_outputs, out_shape=(jax.ShapeDtypeStruct((1, share,...  1.68 us

profile of v7, /device:TPU:0, one launch (start us, length us, event | category | flops | bytes accessed | tf_op | source)
XLA Modules:
  0.0 25.0 jit_solution(16195502744417035057)
XLA Ops:
  0.6 22.7 %shard_map.175 = (f32[64,512]{1,0:T(8,128)}, f32[64,512]{1,0:T(8,128)}, f32[4]{0:T(128)}) custom-call(bf16[512,512]{1,0:T(8,128)(2,1)} %refs_0_.1, bf16[512,128]{1,0:T(8,128)(2,1)} %constant.18.clone.refs_1_, s32[2,4]{1,0:T(2,128)} %bitcast.5, s32[4]{0:T(128)} %refs_3_.1, f32[4]{0:T(128)} %refs_4_.1, f32[2,2,4]{2,1,0:T(2,128)} %bitcast.4, ...), custom_call_target="tpu_custom_call" | custom-call | tf_op jit(solution)/shard_map/pallas_call | solution.py:458
  23.4 1.7 %shard_map.176 = (f32[1,64,512]{2,1,0:T(8,128)}, f32[1,64,512]{2,1,0:T(8,128)}, f32[4]{0:T(128)}) custom-call(f32[64,512]{1,0:T(8,128)} %get-tuple-element.6.image, f32[64,512]{1,0:T(8,128)} %get-tuple-element.7.grad, f32[4]{0:T(128)} %get-tuple-element.8.source), custom_call_target="tpu_custom_call" | custom-call | tf_op jit(solution)/shard_map/pallas_call | solution.py:472

commit v8 on v4

--- a/solution.py
+++ b/solution.py
@@ -323,6 +323,10 @@
         source_out[s] = both_sums[s, 0]
     writes[2].start()
 
+    for step in range(1, n):
+        guarded(lax.rem(me + step, n) < owners, scatter[step].wait_send)
+        guarded(me < owners, gather[step].wait_send)
+
     def stack(value):
         return jnp.concatenate([value, -sign * pltpu.roll(value, K, 1)], 0).astype(jnp.bfloat16)
 
@@ -352,8 +356,6 @@
 
     writes[1].start()
     for step in range(1, n):
-        guarded(lax.rem(me + step, n) < owners, scatter[step].wait_send)
-        guarded(me < owners, gather[step].wait_send)
         spread[step].wait_send()
     for copy in rims:
         copy.wait_send()

time: 24.5 us -> 24.5 us (level)
  no operation moved by 1% of the time
where the time goes in v8:
time: 24.5 us; the launch traced here: 24.3 us
  Pallas kernels  23.7 us (97%)
  between operations  0.64 us (3%)
    pallas_call x1, Pallas kernels, body(): pl.pallas_call(functools.partial(kernel, tuple(order), sizes), out_shape=...  22 us
    pallas_call x1, Pallas kernels, body(): pl.pallas_call(write_outputs, out_shape=(jax.ShapeDtypeStruct((1, share,...  1.68 us

profile of v8, /device:TPU:1, one launch (start us, length us, event | category | flops | bytes accessed | tf_op | source)
XLA Modules:
  0.0 24.3 jit_solution(13213587207768327596)
XLA Ops:
  0.6 22.0 %shard_map.175 = (f32[64,512]{1,0:T(8,128)}, f32[64,512]{1,0:T(8,128)}, f32[4]{0:T(128)}) custom-call(bf16[512,512]{1,0:T(8,128)(2,1)} %refs_0_.1, bf16[512,128]{1,0:T(8,128)(2,1)} %constant.18.clone.refs_1_, s32[2,4]{1,0:T(2,128)} %bitcast.5, s32[4]{0:T(128)} %refs_3_.1, f32[4]{0:T(128)} %refs_4_.1, f32[2,2,4]{2,1,0:T(2,128)} %bitcast.4, ...), custom_call_target="tpu_custom_call" | custom-call | tf_op jit(solution)/shard_map/pallas_call | solution.py:459
  22.7 1.7 %shard_map.176 = (f32[1,64,512]{2,1,0:T(8,128)}, f32[1,64,512]{2,1,0:T(8,128)}, f32[4]{0:T(128)}) custom-call(f32[64,512]{1,0:T(8,128)} %get-tuple-element.6.image, f32[64,512]{1,0:T(8,128)} %get-tuple-element.7.grad, f32[4]{0:T(128)} %get-tuple-element.8.source), custom_call_target="tpu_custom_call" | custom-call | tf_op jit(solution)/shard_map/pallas_call | solution.py:473

commit v9 on v4

--- a/solution.py
+++ b/solution.py
@@ -207,6 +207,10 @@
     def block(index):
         return pl.ds(pl.multiple_of(index * block_rows, block_rows), block_rows)
 
+    def wait_all(slots, sem):
+        taken = slots.at[pl.ds(1, n - 1)]
+        pltpu.make_async_copy(taken, taken, sem.at[0]).wait()
+
     def guarded(condition, run):
         if owners == n:
             run()
@@ -219,7 +223,7 @@
         to = peer if owners == n else jnp.minimum(peer, owners - 1)
         scatter[step] = pltpu.make_async_remote_copy(
             src_ref=part.at[block(to)], dst_ref=landed.at[step],
-            send_sem=scatter_send.at[step], recv_sem=scatter_recv.at[step],
+            send_sem=scatter_send.at[step], recv_sem=scatter_recv.at[0],
             device_id={"src": peer},
         )
         guarded(peer < owners, scatter[step].start)
@@ -227,8 +231,8 @@
 
     def reduce_own():
         acc = part[block(mine), :].astype(jnp.float32)
+        wait_all(landed, scatter_recv)
         for step in range(1, n):
-            scatter[step].wait_recv()
             acc = acc + landed[step].astype(jnp.float32)
         reduced[...] = acc.astype(jnp.bfloat16)
         for step in range(1, n):
@@ -283,7 +287,7 @@
         peer = lax.rem(me + step, n)
         spread[step] = pltpu.make_async_remote_copy(
             src_ref=spec_send, dst_ref=spec_land.at[step],
-            send_sem=spec_ssem.at[step], recv_sem=spec_rsem.at[step],
+            send_sem=spec_ssem.at[step], recv_sem=spec_rsem.at[0],
             device_id={"src": peer},
         )
         spread[step].start()
@@ -327,8 +331,8 @@
         return jnp.concatenate([value, -sign * pltpu.roll(value, K, 1)], 0).astype(jnp.bfloat16)
 
     summed = spec_send[...].astype(jnp.float32)
+    wait_all(spec_land, spec_rsem)
     for step in range(1, n):
-        spread[step].wait_recv()
         summed = summed + spec_land[step].astype(jnp.float32)
     rows = dot(row_back, stack(summed))
     at_rim = jnp.where(tile == 0, me >= n - edges, me < edges)

time: 24.5 us -> 24.5 us (level)
  no operation moved by 1% of the time
where the time goes in v9:
time: 24.5 us; the launch traced here: 24.3 us
  Pallas kernels  23.7 us (97%)
  between operations  0.64 us (3%)
    pallas_call x1, Pallas kernels, body(): pl.pallas_call(functools.partial(kernel, tuple(order), sizes), out_shape=...  22 us
    pallas_call x1, Pallas kernels, body(): pl.pallas_call(write_outputs, out_shape=(jax.ShapeDtypeStruct((1, share,...  1.68 us

profile of v9, /device:TPU:1, one launch (start us, length us, event | category | flops | bytes accessed | tf_op | source)
XLA Modules:
  0.0 24.3 jit_solution(1900811627636364520)
XLA Ops:
  0.6 22.0 %shard_map.175 = (f32[64,512]{1,0:T(8,128)}, f32[64,512]{1,0:T(8,128)}, f32[4]{0:T(128)}) custom-call(bf16[512,512]{1,0:T(8,128)(2,1)} %refs_0_.1, bf16[512,128]{1,0:T(8,128)(2,1)} %constant.18.clone.refs_1_, s32[2,4]{1,0:T(2,128)} %bitcast.5, s32[4]{0:T(128)} %refs_3_.1, f32[4]{0:T(128)} %refs_4_.1, f32[2,2,4]{2,1,0:T(2,128)} %bitcast.4, ...), custom_call_target="tpu_custom_call" | custom-call | tf_op jit(solution)/shard_map/pallas_call | solution.py:461
  22.7 1.7 %shard_map.176 = (f32[1,64,512]{2,1,0:T(8,128)}, f32[1,64,512]{2,1,0:T(8,128)}, f32[4]{0:T(128)}) custom-call(f32[64,512]{1,0:T(8,128)} %get-tuple-element.6.image, f32[64,512]{1,0:T(8,128)} %get-tuple-element.7.grad, f32[4]{0:T(128)} %get-tuple-element.8.source), custom_call_target="tpu_custom_call" | custom-call | tf_op jit(solution)/shard_map/pallas_call | solution.py:475
